TPU v7x, 128 devices: a whole 4x4x4 slice. The times are simulated.
128 devices in a mesh: outer: 4 (over z), inner: 32 (over x, y, core).
Axes of the slice: x: 4, y: 4, z: 4, core: 2. Of those that a mesh axis runs over, the one named last changes fastest.
Arguments:
- query_rows: bfloat16 [16384, 2048], P(('outer', 'inner')), may hold values from -7.1 to 7.1
- key_rows: bfloat16 [16384, 2048], P(('outer', 'inner')), may hold values from -7.1 to 7.1
- value_rows: bfloat16 [16384, 2048], P(('outer', 'inner')), may hold values from -6 to 6
- sample_of: int32 [16384], P(('outer', 'inner')), may hold values from 0 to 7, never falling along the last dimension, each value on 1 to 4096 neighbouring positions
- cotangent: bfloat16 [16384, 2048], P(('outer', 'inner')), may hold values from -6 to 6
Outputs:
- attended: bfloat16 [16384, 2048], P(('outer', 'inner'))
- grad_query: bfloat16 [16384, 2048], P(('outer', 'inner'))
- grad_key: bfloat16 [16384, 2048], P(('outer', 'inner'))
- grad_value: bfloat16 [16384, 2048], P(('outer', 'inner'))
Inputs may be any that keep to these rules, and one draw needn't show every extreme that they name: `sample_of`: sample ids never fall along the tokens; each of the 8 samples holds 1 to 4096 tokens, and one holds exactly 4096.
All inputs are finite; a program needn't handle non-finite values.
Results may differ from a plain program's by a relative error of at most 0.012.
The roundings to bfloat16 on the way count: a program that leaves them out, or rounds other values in their place, can miss the bound.
Values may be sent and summed in bfloat16 or wider, within the bound.
A program may use at most 64 MiB of HBM per device.

v0:
```python
import functools, math
import jax, jax.numpy as jnp
from jax import lax
from jax.sharding import PartitionSpec as P
from jax.experimental import pallas as pl
from jax.experimental.pallas import tpu as pltpu

H, HD, SAMPLES = 32, 64, 8
TQ, TK, ALIGN = 256, 512, 128
PENALTY = -float(2**20)


def attention_kernel(starts, counts, qc_ref, kv_ref, qid_ref, kid_ref, mix_ref, dkv_ref,
                     kaug, kvx, kvT, acc, pbuf, mbuf):
    rows, ext = qc_ref.shape[0], kv_ref.shape[0]
    factor = 1.0 / math.sqrt(HD)
    log2_factor = factor * math.log2(math.e)
    f32, bf16 = jnp.float32, jnp.bfloat16

    def one_hot(ids_row, width):
        sample = lax.broadcasted_iota(jnp.int32, (SAMPLES, width), 0)
        return sample == jnp.broadcast_to(ids_row, (SAMPLES, width))

    def prepare(block, _):
        at = pl.multiple_of(block * TK, TK)
        here = pl.ds(at, TK)
        tile = kv_ref[here, :]
        turned = tile.T
        kvx[here, :] = tile
        kvT[:, here] = turned
        penalty = jnp.where(one_hot(kid_ref[:, here], TK), 0.0, PENALTY)
        penalty = jnp.concatenate([penalty, jnp.zeros((HD - SAMPLES, TK), f32)], axis=0)
        kaug[here, :] = jnp.concatenate([turned[:HD], penalty.astype(bf16)], axis=0).T
        acc[here, :] = jnp.zeros((TK, 2 * HD), f32)
        return 0

    lax.fori_loop(0, ext // TK, prepare, 0)
    pad = pl.ds(ext, TK)
    lane = lax.broadcasted_iota(jnp.int32, (TK, 2 * HD), 1)
    kvx[pad, :] = jnp.zeros((TK, 2 * HD), bf16)
    kvT[:, pad] = jnp.zeros((2 * HD, TK), bf16)
    kaug[pad, :] = jnp.where((lane >= HD) & (lane < HD + SAMPLES), PENALTY, 0.0).astype(bf16)
    acc[pad, :] = jnp.zeros((TK, 2 * HD), f32)

    def query_tile(tile, _):
        q_at = pl.multiple_of(tile * TQ, TQ)
        mine = pl.ds(q_at, TQ)
        qc = qc_ref[mine, :]
        qcT = qc.T
        qT, cT = qcT[:HD], qcT[HD:]
        hot = jnp.where(one_hot(qid_ref[:, mine], TQ), 1.0, 0.0)
        hot = jnp.concatenate([hot, jnp.zeros((HD - SAMPLES, TQ), f32)], axis=0).astype(bf16)
        q_side = jnp.concatenate([qT, hot], axis=0)
        c_side = jnp.concatenate([jnp.zeros_like(cT), cT], axis=0)
        lanes = lax.broadcasted_iota(jnp.int32, qc.shape, 1)
        q_only = jnp.where(lanes < HD, qc, jnp.zeros_like(qc))
        c_only = jnp.where(lanes < HD, jnp.zeros_like(qc), qc)
        cq = jnp.concatenate([c_only, q_only], axis=0)
        first = starts[tile]
        count = counts[tile]

        def key_rows(step):
            return pl.ds(pl.multiple_of(first + step * TK, ALIGN), TK)

        def slot(step):
            return pl.ds(pl.multiple_of(step * TK, TK), TK)

        def score_step(step, state):
            top, total = state
            scores = jnp.dot(kaug[key_rows(step), :], q_side, preferred_element_type=f32) * log2_factor
            new_top = jnp.maximum(top, jnp.max(scores, axis=0, keepdims=True))
            terms = jnp.exp2(scores - new_top)
            pbuf[slot(step), :] = terms
            mbuf[step] = new_top
            return new_top, total * jnp.exp2(top - new_top) + jnp.sum(terms, axis=0, keepdims=True)

        top, total = lax.fori_loop(
            0, count, score_step, (jnp.full((1, TQ), -1e30, f32), jnp.zeros((1, TQ), f32))
        )
        scale = 1.0 / total

        def value_step(step, summed):
            weights = pbuf[slot(step), :] * (jnp.exp2(mbuf[step] - top) * scale)
            return summed + jnp.dot(
                kvT[HD:, key_rows(step)], weights.astype(bf16), preferred_element_type=f32
            )

        mixed = lax.fori_loop(0, count, value_step, jnp.zeros((HD, TQ), f32)).astype(bf16)
        row_dot = jnp.sum(cT.astype(f32) * mixed.astype(f32), axis=0, keepdims=True)

        def grad_step(step, summed):
            keys = key_rows(step)
            weights = pbuf[slot(step), :] * (jnp.exp2(mbuf[step] - top) * scale)
            grad_prob = jnp.dot(kvx[keys, :], c_side, preferred_element_type=f32)
            grad_score = (weights * (grad_prob - row_dot)).astype(bf16)
            pair = jnp.concatenate([weights.astype(bf16), grad_score], axis=1)
            acc[keys, :] += jnp.dot(pair, cq, preferred_element_type=f32)
            return summed + jnp.dot(kvT[:HD, keys], grad_score, preferred_element_type=f32)

        grad_query = lax.fori_loop(0, count, grad_step, jnp.zeros((HD, TQ), f32)) * factor
        mix_ref[mine, :] = jnp.concatenate([mixed, grad_query.astype(bf16)], axis=0).T
        return 0

    lax.fori_loop(0, rows // TQ, query_tile, 0)

    def finish(block, _):
        here = pl.ds(pl.multiple_of(block * TK, TK), TK)
        grads = acc[here, :]
        dkv_ref[here, :] = jnp.where(lane < HD, grads * factor, grads).astype(bf16)
        return 0

    lax.fori_loop(0, ext // TK, finish, 0)


def attention(starts, counts, qc, kv, qid, kid):
    rows, ext = qc.shape[0], kv.shape[0]
    vmem = pl.BlockSpec(memory_space=pltpu.VMEM)
    smem = pl.BlockSpec(memory_space=pltpu.SMEM)
    most = 2 * rows + TQ + TK + ALIGN
    return pl.pallas_call(
        attention_kernel,
        out_shape=(jax.ShapeDtypeStruct((rows, 2 * HD), jnp.bfloat16),
                   jax.ShapeDtypeStruct((ext, 2 * HD), jnp.bfloat16)),
        in_specs=[smem, smem, vmem, vmem, vmem, vmem],
        out_specs=(vmem, vmem),
        scratch_shapes=[
            pltpu.VMEM((ext + TK, 2 * HD), jnp.bfloat16),
            pltpu.VMEM((ext + TK, 2 * HD), jnp.bfloat16),
            pltpu.VMEM((2 * HD, ext + TK), jnp.bfloat16),
            pltpu.VMEM((ext + TK, 2 * HD), jnp.float32),
            pltpu.VMEM(((most + TK - 1) // TK * TK, TQ), jnp.float32),
            pltpu.VMEM(((most + TK - 1) // TK, 1, TQ), jnp.float32),
        ],
        compiler_params=pltpu.CompilerParams(vmem_limit_bytes=56 * 2**20),
        name="attention",
    )(starts, counts, qc, kv, qid, kid)


def on_device(query_rows, key_rows, value_rows, sample_of, cotangent):
    inner = lax.axis_size("inner")
    outer = lax.axis_size("outer")
    tok = query_rows.shape[0]
    rows = tok * inner
    all_ids = lax.all_gather(sample_of, ("outer", "inner"), axis=0, tiled=True)
    group = lax.axis_index("outer")
    padded = jnp.concatenate([jnp.full((rows,), -1, jnp.int32), all_ids, jnp.full((rows,), SAMPLES, jnp.int32)])
    row_ids = lax.dynamic_slice_in_dim(all_ids, group * rows, rows, 0)
    ext_ids = lax.dynamic_slice_in_dim(padded, group * rows, 3 * rows, 0)
    tiles = row_ids.reshape(rows // TQ, TQ)
    low = jnp.sum((ext_ids[None, :] < tiles[:, :1]).astype(jnp.int32), axis=1)
    high = jnp.sum((ext_ids[None, :] <= tiles[:, -1:]).astype(jnp.int32), axis=1)
    starts = low // ALIGN * ALIGN
    counts = (high - starts + TK - 1) // TK

    def pair(a, b):
        a = a.reshape(tok, inner, HD)
        b = b.reshape(tok, inner, HD)
        both = jnp.concatenate([a, b], axis=2)
        return lax.all_to_all(both, "inner", split_axis=1, concat_axis=0, tiled=True).reshape(rows, 2 * HD)

    kv = pair(key_rows, value_rows)
    up = [(i, i + 1) for i in range(outer - 1)]
    down = [(j, i) for i, j in up]
    before = lax.ppermute(kv, "outer", up)
    after = lax.ppermute(kv, "outer", down)
    qc = pair(query_rows, cotangent)
    kv_ext = jnp.concatenate([before, kv, after], axis=0)
    mix, dkv = attention(starts, counts, qc, kv_ext, row_ids[None], ext_ids[None])
    from_above = lax.ppermute(dkv[:rows], "outer", down)
    from_below = lax.ppermute(dkv[2 * rows:], "outer", up)
    total = dkv[rows:2 * rows].astype(jnp.float32) + from_above.astype(jnp.float32) + from_below.astype(jnp.float32)

    def back(both):
        both = lax.all_to_all(both.reshape(rows, 1, 2 * HD), "inner", split_axis=0, concat_axis=1, tiled=True)
        return both[:, :, :HD].reshape(tok, H * HD), both[:, :, HD:].reshape(tok, H * HD)

    attended, grad_query = back(mix)
    grad_key, grad_value = back(total.astype(jnp.bfloat16))
    return attended, grad_query, grad_key, grad_value


def solution(mesh):
    rows = P(("outer", "inner"), None)
    return jax.shard_map(
        on_device, mesh=mesh,
        in_specs=(rows, rows, rows, P(("outer", "inner")), rows),
        out_specs=(rows,) * 4, check_vma=False,
    )
```

profile of v0, /device:TPU:1, one launch (start us, length us, event | category | flops | bytes accessed | tf_op | source)
XLA Modules:
  0.0 295.4 jit_solution(16557167934481255020)
XLA Ops:
  0.6 1.4 copy.72
  2.0 1.3 copy.73
  4.4 8.6 %all-to-all-start.1 = ((bf16[128,32,128]{0,2,1:T(8,128)(2,1)}), bf16[128,32,128]{0,2,1:T(8,128)(2,1)S(1)}, u32[]{:S(2)}, u32[]{:S(2)}) async-start(bf16[128,32,128]{0,2,1:T(8,128)(2,1)} %pad_maximum_fusion.2), calls=%async_computation.1 | async-start | bytes 2097152 | tf_op jit(solution)/shard_map/all_to_all | solution.py:159
  13.3 1.3 copy.70
  14.6 15.3 %all-to-all-done.1 = bf16[128,32,128]{0,2,1:T(8,128)(2,1)S(1)} async-done(((bf16[128,32,128]{0,2,1:T(8,128)(2,1)}), bf16[128,32,128]{0,2,1:T(8,128)(2,1)S(1)}, u32[]{:S(2)}, u32[]{:S(2)}) %all-to-all-start.1) | async-done | bytes 1048608 | tf_op jit(solution)/shard_map/all_to_all | solution.py:159
  30.6 4.5 %collective-permute-start = (bf16[4096,128]{1,0:T(8,128)(2,1)S(1)}, bf16[4096,128]{1,0:T(8,128)(2,1)}, u32[]{:S(2)}, u32[]{:S(2)}) collective-permute-start(bf16[4096,128]{1,0:T(8,128)(2,1)S(1)} %bitcast.38), channel_id=1, source_target_pairs={{0,32},{32,64},{64,96},{1,33},{33,65},{65,97},{2,34},{34,66},{66,9... | collective-permute-start | bytes 3145736 | tf_op jit(solution)/shard_map/ppermute | solution.py:164
  35.1 1.3 collective-permute-start.1
  37.5 4.2 %all-to-all-start = ((bf16[128,32,128]{0,2,1:T(8,128)(2,1)}), bf16[128,32,128]{0,2,1:T(8,128)(2,1)S(1)}, u32[]{:S(2)}, u32[]{:S(2)}) async-start(bf16[128,32,128]{0,2,1:T(8,128)(2,1)} %pad_maximum_fusion.1), calls=%async_computation | async-start | bytes 2097152 | tf_op jit(solution)/shard_map/all_to_all | solution.py:159
  41.8 42.8 %all-gather = s32[128,1,128]{2,1,0:T(1,128)S(1)} all-gather(s32[1,1,128]{2,1,0:T(1,128)S(1)} %bitcast.54), channel_id=1, replica_groups=mesh['outer'=4,'inner'=32] {'outer','inner'}, dimensions={0}, use_global_device_ids=true | all-gather | bytes 66048 | tf_op jit(solution)/shard_map/all_gather | solution.py:144
  85.8 1.3 copy.71
  87.1 9.6 %pad_maximum_fusion.kv_ref = bf16[12288,128]{1,0:T(8,128)(2,1)} fusion(bf16[4096,128]{1,0:T(8,128)(2,1)} %collective-permute-done.1, bf16[4096,128]{1,0:T(8,128)(2,1)S(1)} %bitcast.40, bf16[4096,128]{1,0:T(8,128)(2,1)} %collective-permute-done), kind=kLoop, calls=%fused_computation | loop fusion | flops 9437184 | bytes 6291456 | tf_op jit(solution)/shard_map/concatenate | solution.py:167
  96.7 132.0 %attention.1 = (bf16[4096,128]{1,0:T(8,128)(2,1)}, bf16[12288,128]{1,0:T(8,128)(2,1)}) custom-call(s32[16]{0:T(128)} %get-tuple-element.33.starts, s32[16]{0:T(128)} %get-tuple-element.32.counts, bf16[4096,128]{1,0:T(8,128)(2,1)} %bitcast.35, bf16[12288,128]{1,0:T(8,128)(2,1)} %pad_maximum_fusion.kv_ref, s32[1,4096]{1,0:T(1,128)} %bitcast.53, ...), custom_call_target="tpu_custom_call" | custom-call | tf_op jit(solution)/shard_map/attention/pallas_call | solution.py:120
  228.7 3.2 %fusion.5 = (bf16[4096,128]{1,0:T(8,128)(2,1)}, bf16[4096,128]{1,0:T(8,128)(2,1)}) fusion(bf16[12288,128]{1,0:T(8,128)(2,1)} %get-tuple-element.7), kind=kLoop, calls=%fused_computation.23 | loop fusion | bytes 4194304 | tf_op jit(solution)/shard_map/slice | solution.py:169
  231.8 1.3 collective-permute-start.2
  233.1 5.0 %collective-permute-start.3 = (bf16[4096,128]{1,0:T(8,128)(2,1)}, bf16[4096,128]{1,0:T(8,128)(2,1)}, u32[]{:S(2)}, u32[]{:S(2)}) collective-permute-start(bf16[4096,128]{1,0:T(8,128)(2,1)} %get-tuple-element.35), channel_id=1, source_target_pairs={{0,32},{32,64},{64,96},{1,33},{33,65},{65,97},{2,34},{34,66},{66,9... | collective-permute-start | bytes 3145736 | tf_op jit(solution)/shard_map/ppermute | solution.py:170
  238.6 1.4 reduce.4
  240.0 1.1 reshape.67
  241.2 5.8 %all-to-all-start.2 = ((bf16[32,2,8192]{2,1,0:T(2,128)(2,1)}), bf16[32,2,8192]{2,1,0:T(2,128)(2,1)S(1)}, u32[]{:S(2)}, u32[]{:S(2)}) async-start(bf16[32,2,8192]{2,1,0:T(2,128)(2,1)} %reshape.67), calls=%async_computation.2 | async-start | bytes 2097152 | tf_op jit(solution)/shard_map/all_to_all | solution.py:174
  247.0 11.6 %collective-permute-done.2 = bf16[4096,128]{1,0:T(8,128)(2,1)S(1)} collective-permute-done((bf16[4096,128]{1,0:T(8,128)(2,1)}, bf16[4096,128]{1,0:T(8,128)(2,1)S(1)}, u32[]{:S(2)}, u32[]{:S(2)}) %collective-permute-start.2) | collective-permute-done | bytes 1048608 | tf_op jit(solution)/shard_map/ppermute | solution.py:169
  259.5 2.3 fusion
  261.8 1.4 reduce.5
  264.3 6.4 %all-to-all-start.3 = ((bf16[32,2,8192]{2,1,0:T(2,128)(2,1)}), bf16[32,2,8192]{2,1,0:T(2,128)(2,1)}, u32[]{:S(2)}, u32[]{:S(2)}) async-start(bf16[32,2,8192]{2,1,0:T(2,128)(2,1)} %reshape.69), calls=%async_computation.3 | async-start | bytes 2097152 | tf_op jit(solution)/shard_map/all_to_all | solution.py:174
  275.2 12.5 %all-to-all-done.3 = bf16[32,2,8192]{2,1,0:T(2,128)(2,1)} async-done(((bf16[32,2,8192]{2,1,0:T(2,128)(2,1)}), bf16[32,2,8192]{2,1,0:T(2,128)(2,1)}, u32[]{:S(2)}, u32[]{:S(2)}) %all-to-all-start.3) | async-done | bytes 1048608 | tf_op jit(solution)/shard_map/all_to_all | solution.py:174
  287.7 4.3 %reshape.70 = bf16[4096,1,128]{2,1,0:T(2,128)(2,1)S(1)} reshape(bf16[32,2,8192]{2,1,0:T(2,128)(2,1)} %all-to-all-done.3) | data formatting | bytes 2097152
  (44 shorter events, 14.7 us)
Async XLA Ops:
  0.6 12.4 %copy-start.2 = (bf16[128,2048]{1,0:T(8,128)(2,1)S(1)}, bf16[128,2048]{1,0:T(8,128)(2,1)}, u32[]{:S(2)}) copy-start(bf16[128,2048]{1,0:T(8,128)(2,1)} %param.5) | copy-start | bytes 1572868
  4.4 25.5 %all-to-all-start.1 = ((bf16[128,32,128]{0,2,1:T(8,128)(2,1)}), bf16[128,32,128]{0,2,1:T(8,128)(2,1)S(1)}, u32[]{:S(2)}, u32[]{:S(2)}) async-start(bf16[128,32,128]{0,2,1:T(8,128)(2,1)} %pad_maximum_fusion.2), calls=%async_computation.1 | async-start | bytes 2097152 | tf_op jit(solution)/shard_map/all_to_all | solution.py:159
  29.9 11.8 %copy-start.5 = (s32[128]{0:T(128)S(1)}, s32[128]{0:T(128)}, u32[]{:S(2)}) copy-start(s32[128]{0:T(128)} %param.8) | copy-start | bytes 1540
  30.6 56.5 %collective-permute-start = (bf16[4096,128]{1,0:T(8,128)(2,1)S(1)}, bf16[4096,128]{1,0:T(8,128)(2,1)}, u32[]{:S(2)}, u32[]{:S(2)}) collective-permute-start(bf16[4096,128]{1,0:T(8,128)(2,1)S(1)} %bitcast.38), channel_id=1, source_target_pairs={{0,32},{32,64},{64,96},{1,33},{33,65},{65,97},{2,34},{34,66},{66,9... | collective-permute-start | bytes 3145736 | tf_op jit(solution)/shard_map/ppermute | solution.py:164
  35.1 52.0 %collective-permute-start.1 = (bf16[4096,128]{1,0:T(8,128)(2,1)S(1)}, bf16[4096,128]{1,0:T(8,128)(2,1)}, u32[]{:S(2)}, u32[]{:S(2)}) collective-permute-start(bf16[4096,128]{1,0:T(8,128)(2,1)S(1)} %bitcast.39), channel_id=1, source_target_pairs={{32,0},{64,32},{96,64},{33,1},{65,33},{97,65},{34,2},{66,34},{98,6... | collective-permute-start | bytes 3145736 | tf_op jit(solution)/shard_map/ppermute | solution.py:165
  37.5 48.3 %all-to-all-start = ((bf16[128,32,128]{0,2,1:T(8,128)(2,1)}), bf16[128,32,128]{0,2,1:T(8,128)(2,1)S(1)}, u32[]{:S(2)}, u32[]{:S(2)}) async-start(bf16[128,32,128]{0,2,1:T(8,128)(2,1)} %pad_maximum_fusion.1), calls=%async_computation | async-start | bytes 2097152 | tf_op jit(solution)/shard_map/all_to_all | solution.py:159
  84.6 12.1 %copy-start.4 = (s32[4096]{0:T(1024)}, s32[4096]{0:T(1024)S(1)}, u32[]{:S(2)}) copy-start(s32[4096]{0:T(1024)S(1)} %dynamic_slice.7) | copy-start | bytes 49156
  84.8 11.9 %copy-start.3 = (s32[12288]{0:T(1024)}, s32[12288]{0:T(1024)S(1)}, u32[]{:S(2)}) copy-start(s32[12288]{0:T(1024)S(1)} %fusion.2) | copy-start | bytes 147460
  228.7 9.9 %copy-start = (bf16[4096,128]{1,0:T(8,128)(2,1)S(1)}, bf16[4096,128]{1,0:T(8,128)(2,1)}, u32[]{:S(2)}) copy-start(bf16[4096,128]{1,0:T(8,128)(2,1)} %get-tuple-element.6) | copy-start | bytes 3145732
  231.8 26.7 %collective-permute-start.2 = (bf16[4096,128]{1,0:T(8,128)(2,1)}, bf16[4096,128]{1,0:T(8,128)(2,1)S(1)}, u32[]{:S(2)}, u32[]{:S(2)}) collective-permute-start(bf16[4096,128]{1,0:T(8,128)(2,1)} %get-tuple-element.34), channel_id=1, source_target_pairs={{32,0},{64,32},{96,64},{33,1},{65,33},{97,65},{34,2},{66,34},{98,6... | collective-permute-start | bytes 3145736 | tf_op jit(solution)/shard_map/ppermute | solution.py:169
  233.1 26.4 %collective-permute-start.3 = (bf16[4096,128]{1,0:T(8,128)(2,1)}, bf16[4096,128]{1,0:T(8,128)(2,1)}, u32[]{:S(2)}, u32[]{:S(2)}) collective-permute-start(bf16[4096,128]{1,0:T(8,128)(2,1)} %get-tuple-element.35), channel_id=1, source_target_pairs={{0,32},{32,64},{64,96},{1,33},{33,65},{65,97},{2,34},{34,66},{66,9... | collective-permute-start | bytes 3145736 | tf_op jit(solution)/shard_map/ppermute | solution.py:170
  241.2 23.2 %all-to-all-start.2 = ((bf16[32,2,8192]{2,1,0:T(2,128)(2,1)}), bf16[32,2,8192]{2,1,0:T(2,128)(2,1)S(1)}, u32[]{:S(2)}, u32[]{:S(2)}) async-start(bf16[32,2,8192]{2,1,0:T(2,128)(2,1)} %reshape.67), calls=%async_computation.2 | async-start | bytes 2097152 | tf_op jit(solution)/shard_map/all_to_all | solution.py:174
  258.5 1.0 copy-start.1
  264.3 23.3 %all-to-all-start.3 = ((bf16[32,2,8192]{2,1,0:T(2,128)(2,1)}), bf16[32,2,8192]{2,1,0:T(2,128)(2,1)}, u32[]{:S(2)}, u32[]{:S(2)}) async-start(bf16[32,2,8192]{2,1,0:T(2,128)(2,1)} %reshape.69), calls=%async_computation.3 | async-start | bytes 2097152 | tf_op jit(solution)/shard_map/all_to_all | solution.py:174
where the time goes:
time: 296 us; the launch traced here: 295 us
  Pallas kernels  132 us (45%)
  blocking collectives  42.8 us (14%)
  waiting for transfers between devices  39.4 us (13%)
  starting transfers between devices  37 us (12%)
  local copies, waits for them, and re-layouts  25.5 us (9%)
  other arithmetic  17.9 us (6%)
    pallas_call x1, Pallas kernels, attention(): pl.pallas_call(attention_kernel, out_shape=(jax.ShapeDtypeStruct((rows, 2...  132 us
    all_gather x1, blocking collectives, on_device(): all_ids = lax.all_gather(sample_of, ('outer', 'inner'), axis=0, tiled=True)  42.8 us
    unnamed x26, local copies, waits for them, and re-layouts  17.2 us
    all_to_all x2, waiting for transfers between devices, pair(): lax.all_to_all(both, 'inner', split_axis=1, concat_axis=0, tiled=True)  15.3 us
    all_to_all x2, starting transfers between devices, pair(): lax.all_to_all(both, 'inner', split_axis=1, concat_axis=0, tiled=True)  12.8 us
    all_to_all x2, waiting for transfers between devices, back(): lax.all_to_all(both.reshape(rows, 1, 2 * HD), 'inner', split_axis=0, conc...  12.5 us
    all_to_all x2, starting transfers between devices, back(): lax.all_to_all(both.reshape(rows, 1, 2 * HD), 'inner', split_axis=0, conc...  12.2 us
    ppermute x1, waiting for transfers between devices, on_device(): from_above = lax.ppermute(dkv[:rows], 'outer', down)  11.6 us
  transfers between devices with their start and end apart: 8, of which 3 were waited for; matrix products, arithmetic and copies ran while one was open for 6% of the time, Pallas kernels for 0%

commit v1 on v0

--- a/solution.py
+++ b/solution.py
@@ -6,7 +6,7 @@
 from jax.experimental.pallas import tpu as pltpu
 
 H, HD, SAMPLES = 32, 64, 8
-TQ, TK, ALIGN = 256, 512, 128
+TQ, TK, ALIGN = 512, 512, 128
 PENALTY = -float(2**20)
 
 
@@ -136,47 +136,361 @@
     )(starts, counts, qc, kv, qid, kid)
 
 
+LANES = 2 * HD
+MESH = pl.DeviceIdType.MESH
+
+
+def partner(me, hop, size):
+    return lax.rem(me + hop, size)
+
+
+def packed(first, second, head):
+    columns = slice(head * HD, (head + 1) * HD)
+    return jnp.concatenate([first[:, columns], second[:, columns]], axis=1)
+
+
+def collect_kernel(size, planes, q_ref, k_ref, v_ref, c_ref, id_ref, qc_ref, kv_ref, ids_ref,
+                   qc_pack, kv_pack, own_sem, kv_send, kv_recv, qc_send, qc_recv,
+                   id_send, id_recv, z_send, z_recv, zid_send, zid_recv):
+    me, plane = lax.axis_index("inner"), lax.axis_index("outer")
+    tok = q_ref.shape[0]
+    rows = tok * size
+    chunks = z_send.shape[1]
+    share = size // chunks
+    above, below = partner(plane, 1, planes), partner(plane, planes - 1, planes)
+
+    barrier = pltpu.get_barrier_semaphore()
+
+    def greet(hop, _):
+        pl.semaphore_signal(barrier, inc=1, device_id={"inner": partner(me, hop, size)}, device_id_type=MESH)
+        return 0
+
+    lax.fori_loop(1, size, greet, 0)
+    for other in (above, below):
+        pl.semaphore_signal(barrier, inc=1, device_id={"outer": other}, device_id_type=MESH)
+    for head in range(size):
+        kv_pack[head] = packed(k_ref, v_ref, head)
+    pl.semaphore_wait(barrier, size + 1)
+
+    def block(owner, base=0):
+        return pl.ds(pl.multiple_of(base + owner * tok, tok), tok)
+
+    def kv_copy(other, slot):
+        return pltpu.make_async_remote_copy(
+            src_ref=kv_pack.at[other], dst_ref=kv_ref.at[block(slot, rows)],
+            send_sem=kv_send.at[other], recv_sem=kv_recv.at[slot],
+            device_id={"inner": other}, device_id_type=MESH)
+
+    def qc_copy(other, slot):
+        return pltpu.make_async_remote_copy(
+            src_ref=qc_pack.at[other], dst_ref=qc_ref.at[block(slot)],
+            send_sem=qc_send.at[other], recv_sem=qc_recv.at[slot],
+            device_id={"inner": other}, device_id_type=MESH)
+
+    def id_copy(other, slot):
+        return pltpu.make_async_remote_copy(
+            src_ref=id_ref, dst_ref=ids_ref.at[1, pl.ds(slot, 1)],
+            send_sem=id_send.at[other], recv_sem=id_recv.at[slot],
+            device_id={"inner": other}, device_id_type=MESH)
+
+    own_kv = pltpu.make_async_copy(kv_pack.at[me], kv_ref.at[block(me, rows)], own_sem.at[0])
+    own_id = pltpu.make_async_copy(id_ref, ids_ref.at[1, pl.ds(me, 1)], own_sem.at[1])
+    own_kv.start()
+    own_id.start()
+
+    def send_kv(hop, _):
+        other = partner(me, hop, size)
+        kv_copy(other, me).start()
+        id_copy(other, me).start()
+        return 0
+
+    lax.fori_loop(1, size, send_kv, 0)
+    for head in range(size):
+        qc_pack[head] = packed(q_ref, c_ref, head)
+    own_qc = pltpu.make_async_copy(qc_pack.at[me], qc_ref.at[block(me)], own_sem.at[2])
+    own_qc.start()
+
+    def send_qc(hop, _):
+        qc_copy(partner(me, hop, size), me).start()
+        return 0
+
+    lax.fori_loop(1, size, send_qc, 0)
+
+    own_kv.wait()
+    own_id.wait()
+
+    def z_copies(chunk):
+        src = kv_ref.at[pl.ds(pl.multiple_of(rows + chunk * (share * tok), share * tok), share * tok)]
+        up = pltpu.make_async_remote_copy(
+            src_ref=src, dst_ref=kv_ref.at[pl.ds(pl.multiple_of(chunk * (share * tok), share * tok), share * tok)],
+            send_sem=z_send.at[0, chunk], recv_sem=z_recv.at[0, chunk],
+            device_id={"outer": above}, device_id_type=MESH)
+        down = pltpu.make_async_remote_copy(
+            src_ref=src, dst_ref=kv_ref.at[pl.ds(pl.multiple_of(2 * rows + chunk * (share * tok), share * tok), share * tok)],
+            send_sem=z_send.at[1, chunk], recv_sem=z_recv.at[1, chunk],
+            device_id={"outer": below}, device_id_type=MESH)
+        return up, down
+
+    home = me // share
+
+    def pass_on(step, _):
+        chunk = lax.rem(home + chunks - step, chunks)
+
+        def arrive(i, _):
+            slot = chunk * share + i
+
+            @pl.when(slot != me)
+            def _():
+                kv_copy(slot, slot).wait_recv()
+
+            return 0
+
+        lax.fori_loop(0, share, arrive, 0)
+        for copy in z_copies(chunk):
+            copy.start()
+        return 0
+
+    lax.fori_loop(0, chunks, pass_on, 0)
+
+    def id_arrive(hop, _):
+        slot = partner(me, hop, size)
+        id_copy(slot, slot).wait_recv()
+        return 0
+
+    lax.fori_loop(1, size, id_arrive, 0)
+    id_up = pltpu.make_async_remote_copy(
+        src_ref=ids_ref.at[1], dst_ref=ids_ref.at[0], send_sem=zid_send.at[0], recv_sem=zid_recv.at[0],
+        device_id={"outer": above}, device_id_type=MESH)
+    id_down = pltpu.make_async_remote_copy(
+        src_ref=ids_ref.at[1], dst_ref=ids_ref.at[2], send_sem=zid_send.at[1], recv_sem=zid_recv.at[1],
+        device_id={"outer": below}, device_id_type=MESH)
+    id_up.start()
+    id_down.start()
+
+    own_qc.wait()
+
+    def settle(hop, _):
+        slot = partner(me, hop, size)
+        qc_copy(slot, slot).wait_recv()
+        kv_copy(slot, me).wait_send()
+        qc_copy(slot, me).wait_send()
+        id_copy(slot, me).wait_send()
+        return 0
+
+    lax.fori_loop(1, size, settle, 0)
+    id_up.wait()
+    id_down.wait()
+
+    def settle_z(chunk, _):
+        for copy in z_copies(chunk):
+            copy.wait()
+        return 0
+
+    lax.fori_loop(0, chunks, settle_z, 0)
+
+
+def collect(size, planes, q, k, v, c, ids):
+    tok = q.shape[0]
+    rows = tok * size
+    vmem = pl.BlockSpec(memory_space=pltpu.VMEM)
+    hbm = pl.BlockSpec(memory_space=pl.ANY)
+    dma = pltpu.SemaphoreType.DMA
+    chunks = 8
+    return pl.pallas_call(
+        functools.partial(collect_kernel, size, planes),
+        out_shape=(jax.ShapeDtypeStruct((rows, LANES), jnp.bfloat16),
+                   jax.ShapeDtypeStruct((3 * rows, LANES), jnp.bfloat16),
+                   jax.ShapeDtypeStruct((3, size, tok), jnp.int32)),
+        in_specs=[vmem] * 5,
+        out_specs=(hbm, hbm, vmem),
+        scratch_shapes=[
+            pltpu.VMEM((size, tok, LANES), jnp.bfloat16),
+            pltpu.VMEM((size, tok, LANES), jnp.bfloat16),
+            dma((3,)), dma((size,)), dma((size,)), dma((size,)), dma((size,)),
+            dma((size,)), dma((size,)), dma((2, chunks)), dma((2, chunks)), dma((2,)), dma((2,)),
+        ],
+        compiler_params=pltpu.CompilerParams(collective_id=0, has_side_effects=True, vmem_limit_bytes=32 * 2**20),
+        name="collect",
+    )(q, k, v, c, ids)
+
+
+def return_kernel(size, planes, mix_ref, dkv_ref, rmix_ref, rkv_ref, from_z, total,
+                  own_sem, mix_send, mix_recv, kv_send, kv_recv, z_send, z_recv):
+    me, plane = lax.axis_index("inner"), lax.axis_index("outer")
+    rows = mix_ref.shape[0]
+    tok = rows // size
+    chunks = z_send.shape[1]
+    share = size // chunks
+    step_rows = share * tok
+    above, below = partner(plane, 1, planes), partner(plane, planes - 1, planes)
+    barrier = pltpu.get_barrier_semaphore()
+
+    def greet(hop, _):
+        pl.semaphore_signal(barrier, inc=1, device_id={"inner": partner(me, hop, size)}, device_id_type=MESH)
+        return 0
+
+    lax.fori_loop(1, size, greet, 0)
+    for other in (above, below):
+        pl.semaphore_signal(barrier, inc=1, device_id={"outer": other}, device_id_type=MESH)
+    pl.semaphore_wait(barrier, size + 1)
+
+    def block(owner):
+        return pl.ds(pl.multiple_of(owner * tok, tok), tok)
+
+    def part(chunk, base=0):
+        return pl.ds(pl.multiple_of(base + chunk * step_rows, step_rows), step_rows)
+
+    def z_copies(chunk):
+        down = pltpu.make_async_remote_copy(
+            src_ref=dkv_ref.at[part(chunk)], dst_ref=from_z.at[0, part(chunk)],
+            send_sem=z_send.at[0, chunk], recv_sem=z_recv.at[0, chunk],
+            device_id={"outer": below}, device_id_type=MESH)
+        up = pltpu.make_async_remote_copy(
+            src_ref=dkv_ref.at[part(chunk, 2 * rows)], dst_ref=from_z.at[1, part(chunk)],
+            send_sem=z_send.at[1, chunk], recv_sem=z_recv.at[1, chunk],
+            device_id={"outer": above}, device_id_type=MESH)
+        return down, up
+
+    def mix_copy(other, slot):
+        return pltpu.make_async_remote_copy(
+            src_ref=mix_ref.at[block(other)], dst_ref=rmix_ref.at[slot],
+            send_sem=mix_send.at[other], recv_sem=mix_recv.at[slot],
+            device_id={"inner": other}, device_id_type=MESH)
+
+    def kv_copy(other, slot):
+        return pltpu.make_async_remote_copy(
+            src_ref=total.at[block(other)], dst_ref=rkv_ref.at[slot],
+            send_sem=kv_send.at[other], recv_sem=kv_recv.at[slot],
+            device_id={"inner": other}, device_id_type=MESH)
+
+    home = me // share
+
+    def send_z(step, _):
+        for copy in z_copies(lax.rem(home + step, chunks)):
+            copy.start()
+        return 0
+
+    lax.fori_loop(0, chunks, send_z, 0)
+    own_mix = pltpu.make_async_copy(mix_ref.at[block(me)], rmix_ref.at[me], own_sem.at[0])
+    own_mix.start()
+
+    def send_mix(hop, _):
+        mix_copy(partner(me, hop, size), me).start()
+        return 0
+
+    lax.fori_loop(1, size, send_mix, 0)
+    own_kv = pltpu.make_async_copy(total.at[block(me)], rkv_ref.at[me], own_sem.at[1])
+
+    def add_up(step, _):
+        chunk = lax.rem(home + step, chunks)
+        for copy in z_copies(chunk):
+            copy.wait_recv()
+        mine = dkv_ref[part(chunk, rows), :].astype(jnp.float32)
+        first = from_z[0, part(chunk), :].astype(jnp.float32)
+        second = from_z[1, part(chunk), :].astype(jnp.float32)
+        total[part(chunk), :] = (mine + first + second).astype(jnp.bfloat16)
+
+        def send(i, _):
+            other = chunk * share + i
+
+            @pl.when(other != me)
+            def _():
+                kv_copy(other, me).start()
+
+            @pl.when(other == me)
+            def _():
+                own_kv.start()
+
+            return 0
+
+        lax.fori_loop(0, share, send, 0)
+        return 0
+
+    lax.fori_loop(0, chunks, add_up, 0)
+    own_mix.wait()
+    own_kv.wait()
+
+    def settle(hop, _):
+        slot = partner(me, hop, size)
+        mix_copy(slot, slot).wait_recv()
+        kv_copy(slot, slot).wait_recv()
+        mix_copy(slot, me).wait_send()
+        kv_copy(slot, me).wait_send()
+        return 0
+
+    lax.fori_loop(1, size, settle, 0)
+
+    def settle_z(chunk, _):
+        for copy in z_copies(chunk):
+            copy.wait_send()
+        return 0
+
+    lax.fori_loop(0, chunks, settle_z, 0)
+
+
+def give_back(size, planes, mix, dkv):
+    rows = mix.shape[0]
+    tok = rows // size
+    vmem = pl.BlockSpec(memory_space=pltpu.VMEM)
+    hbm = pl.BlockSpec(memory_space=pl.ANY)
+    dma = pltpu.SemaphoreType.DMA
+    chunks = 8
+    got = jax.ShapeDtypeStruct((size, tok, LANES), jnp.bfloat16)
+    return pl.pallas_call(
+        functools.partial(return_kernel, size, planes),
+        out_shape=(got, got),
+        in_specs=[vmem, vmem],
+        out_specs=(hbm, hbm),
+        scratch_shapes=[
+            pltpu.VMEM((2, rows, LANES), jnp.bfloat16),
+            pltpu.VMEM((rows, LANES), jnp.bfloat16),
+            dma((2,)), dma((size,)), dma((size,)), dma((size,)), dma((size,)), dma((2, chunks)), dma((2, chunks)),
+        ],
+        compiler_params=pltpu.CompilerParams(collective_id=1, has_side_effects=True, vmem_limit_bytes=32 * 2**20),
+        name="give_back",
+    )(mix, dkv)
+
+
+def unpack_kernel(rmix_ref, rkv_ref, att_ref, dq_ref, dk_ref, dv_ref):
+    for head in range(rmix_ref.shape[0]):
+        columns = slice(head * HD, (head + 1) * HD)
+        mix, grads = rmix_ref[head], rkv_ref[head]
+        att_ref[:, columns] = mix[:, :HD]
+        dq_ref[:, columns] = mix[:, HD:]
+        dk_ref[:, columns] = grads[:, :HD]
+        dv_ref[:, columns] = grads[:, HD:]
+
+
+def unpack(rmix, rkv):
+    heads, tok, _ = rmix.shape
+    vmem = pl.BlockSpec(memory_space=pltpu.VMEM)
+    return pl.pallas_call(
+        unpack_kernel,
+        out_shape=(jax.ShapeDtypeStruct((tok, heads * HD), jnp.bfloat16),) * 4,
+        in_specs=[vmem, vmem],
+        out_specs=(vmem,) * 4,
+        compiler_params=pltpu.CompilerParams(vmem_limit_bytes=32 * 2**20),
+        name="unpack",
+    )(rmix, rkv)
+
+
 def on_device(query_rows, key_rows, value_rows, sample_of, cotangent):
-    inner = lax.axis_size("inner")
-    outer = lax.axis_size("outer")
+    size, planes = lax.axis_size("inner"), lax.axis_size("outer")
     tok = query_rows.shape[0]
-    rows = tok * inner
-    all_ids = lax.all_gather(sample_of, ("outer", "inner"), axis=0, tiled=True)
+    rows = tok * size
+    qc, kv, ids = collect(size, planes, query_rows, key_rows, value_rows, cotangent, sample_of[None])
     group = lax.axis_index("outer")
-    padded = jnp.concatenate([jnp.full((rows,), -1, jnp.int32), all_ids, jnp.full((rows,), SAMPLES, jnp.int32)])
-    row_ids = lax.dynamic_slice_in_dim(all_ids, group * rows, rows, 0)
-    ext_ids = lax.dynamic_slice_in_dim(padded, group * rows, 3 * rows, 0)
+    before = jnp.where(group == 0, -1, ids[0])
+    after = jnp.where(group == planes - 1, SAMPLES, ids[2])
+    row_ids = ids[1].reshape(rows)
+    ext_ids = jnp.concatenate([before.reshape(rows), row_ids, after.reshape(rows)])
     tiles = row_ids.reshape(rows // TQ, TQ)
     low = jnp.sum((ext_ids[None, :] < tiles[:, :1]).astype(jnp.int32), axis=1)
     high = jnp.sum((ext_ids[None, :] <= tiles[:, -1:]).astype(jnp.int32), axis=1)
     starts = low // ALIGN * ALIGN
     counts = (high - starts + TK - 1) // TK
-
-    def pair(a, b):
-        a = a.reshape(tok, inner, HD)
-        b = b.reshape(tok, inner, HD)
-        both = jnp.concatenate([a, b], axis=2)
-        return lax.all_to_all(both, "inner", split_axis=1, concat_axis=0, tiled=True).reshape(rows, 2 * HD)
-
-    kv = pair(key_rows, value_rows)
-    up = [(i, i + 1) for i in range(outer - 1)]
-    down = [(j, i) for i, j in up]
-    before = lax.ppermute(kv, "outer", up)
-    after = lax.ppermute(kv, "outer", down)
-    qc = pair(query_rows, cotangent)
-    kv_ext = jnp.concatenate([before, kv, after], axis=0)
-    mix, dkv = attention(starts, counts, qc, kv_ext, row_ids[None], ext_ids[None])
-    from_above = lax.ppermute(dkv[:rows], "outer", down)
-    from_below = lax.ppermute(dkv[2 * rows:], "outer", up)
-    total = dkv[rows:2 * rows].astype(jnp.float32) + from_above.astype(jnp.float32) + from_below.astype(jnp.float32)
-
-    def back(both):
-        both = lax.all_to_all(both.reshape(rows, 1, 2 * HD), "inner", split_axis=0, concat_axis=1, tiled=True)
-        return both[:, :, :HD].reshape(tok, H * HD), both[:, :, HD:].reshape(tok, H * HD)
-
-    attended, grad_query = back(mix)
-    grad_key, grad_value = back(total.astype(jnp.bfloat16))
-    return attended, grad_query, grad_key, grad_value
+    mix, dkv = attention(starts, counts, qc, kv, row_ids[None], ext_ids[None])
+    return unpack(*give_back(size, planes, mix, dkv))
 
 
 def solution(mesh):

time: 296 us -> 211 us (0.71)
  Pallas kernels: 132 us -> 198 us
  blocking collectives: 42.8 us -> 0 us
  waiting for transfers between devices: 39.4 us -> 0 us
  starting transfers between devices: 37 us -> 0 us
  other arithmetic: 17.9 us -> 0.87 us
  local copies, waits for them, and re-layouts: 25.5 us -> 10.8 us
    pallas_call x0 -> x3, Pallas kernels: none -> 122 us  [the longest x1 76.7 us: give_back(): pl.pallas_call(functools.partial(return_kernel, size, planes), out_shape=...]
    pallas_call x1, Pallas kernels: 132 us -> 76.3 us  [attention(): pl.pallas_call(attention_kernel, out_shape=(jax.ShapeDtypeStruct((rows, 2...]
    all_gather x1 -> x0, blocking collectives: 42.8 us -> none  [on_device(): all_ids = lax.all_gather(sample_of, ('outer', 'inner'), axis=0, tiled=True)]
    all_to_all x4 -> x0, waiting for transfers between devices: 27.8 us -> none  [the longest x2 15.3 us: pair(): lax.all_to_all(both, 'inner', split_axis=1, concat_axis=0, tiled=True)]
    all_to_all x4 -> x0, starting transfers between devices: 25 us -> none  [the longest x2 12.8 us: pair(): lax.all_to_all(both, 'inner', split_axis=1, concat_axis=0, tiled=True)]
    ppermute x4 -> x0, starting transfers between devices: 12 us -> none  [the longest x1 4.96 us: on_device(): from_below = lax.ppermute(dkv[2 * rows:], 'outer', up)]
    concatenate x4 -> x1, other arithmetic: 11.8 us -> 0.01 us  [on_device(): jnp.concatenate([before.reshape(rows), row_ids, after.reshape(rows)])]
    ppermute x4 -> x0, waiting for transfers between devices: 11.6 us -> none  [the longest x1 11.6 us: on_device(): from_above = lax.ppermute(dkv[:rows], 'outer', down)]
  transfers between devices with their start and end apart: 8 -> 0, of which waited for: 3 -> 0; matrix products, arithmetic and copies ran while one was open for 6% -> 0% of each run, Pallas kernels for 0% -> 0%
where the time goes in v1:
time: 211 us
  Pallas kernels  198 us (94%)
  local copies, waits for them, and re-layouts  10.8 us (5%)
    pallas_call x1, Pallas kernels, give_back(): pl.pallas_call(functools.partial(return_kernel, size, planes), out_shape=...  76.7 us
    pallas_call x1, Pallas kernels, attention(): pl.pallas_call(attention_kernel, out_shape=(jax.ShapeDtypeStruct((rows, 2...  76.3 us
    pallas_call x1, Pallas kernels, collect(): pl.pallas_call(functools.partial(collect_kernel, size, planes), out_shape...  42.8 us
    unnamed x24, local copies, waits for them, and re-layouts  10.7 us

profile of v1, /device:TPU:1, one launch (start us, length us, event | category | flops | bytes accessed | tf_op | source)
XLA Modules:
  0.0 210.6 jit_solution(17460758862884345137)
XLA Ops:
  0.6 0.0 copy-start.4
  0.7 1.0 copy-done.4
  1.7 0.0 copy-start.5
  1.7 1.0 copy-done.5
  2.7 1.0 copy-done.6
  3.8 1.0 copy-done.7
  4.8 0.7 copy-done.8
  5.5 42.8 %collect.1 = (bf16[4096,128]{1,0:T(8,128)(2,1)S(1)}, bf16[12288,128]{1,0:T(8,128)(2,1)S(1)}, s32[3,32,128]{2,1,0:T(8,128)S(1)}) custom-call(bf16[128,2048]{1,0:T(8,128)(2,1)S(1)} %copy-done.4, bf16[128,2048]{1,0:T(8,128)(2,1)S(1)} %copy-done.5, bf16[128,2048]{1,0:T(8,128)(2,1)S(1)} %copy-done.6, bf16[128,2048]{1,0:T(8,128)(2,1)S(1)} %copy-done.7, ...), custom_call_target="tpu_custom_call" | custom-call | tf_op jit(solution)/shard_map/collect/pallas_call | solution.py:299
  48.3 0.0 copy-start
  48.3 1.6 copy-done
  49.9 1.0 copy-done.2
  50.9 0.0 copy-start.9
  50.9 0.1 fusion.3
  51.0 0.1 copy.13
  51.1 0.1 copy.14
  51.2 0.3 convert_reduce_fusion
  51.5 0.5 and_select_fusion
  52.0 0.0 copy-done.10
  52.0 0.0 copy-done.9
  52.0 76.3 %attention.1 = (bf16[4096,128]{1,0:T(8,128)(2,1)}, bf16[12288,128]{1,0:T(8,128)(2,1)}) custom-call(s32[8]{0:T(128)} %get-tuple-element.21.starts, s32[8]{0:T(128)} %get-tuple-element.20.counts, bf16[4096,128]{1,0:T(8,128)(2,1)} %copy-done.2, bf16[12288,128]{1,0:T(8,128)(2,1)} %copy-done, s32[1,4096]{1,0:T(1,128)} %bitcast.13, s32[1,12288]{1,0:T(1,128)} %bitcast.12), custom_call_target="tpu_custom_call" | custom-call | tf_op jit(solution)/shard_map/attention/pallas_call | solution.py:120
  128.3 1.9 copy-done.1
  130.2 1.2 copy-done.3
  131.4 76.7 %give_back.1 = (bf16[32,128,128]{2,1,0:T(8,128)(2,1)S(1)}, bf16[32,128,128]{2,1,0:T(8,128)(2,1)S(1)}) custom-call(bf16[4096,128]{1,0:T(8,128)(2,1)S(1)} %copy-done.3, bf16[12288,128]{1,0:T(8,128)(2,1)S(1)} %copy-done.1), custom_call_target="tpu_custom_call" | custom-call | tf_op jit(solution)/shard_map/give_back/pallas_call | solution.py:439
  208.1 2.5 %unpack.1 = (bf16[128,2048]{1,0:T(8,128)(2,1)}, bf16[128,2048]{1,0:T(8,128)(2,1)}, bf16[128,2048]{1,0:T(8,128)(2,1)}, bf16[128,2048]{1,0:T(8,128)(2,1)}) custom-call(bf16[32,128,128]{2,1,0:T(8,128)(2,1)S(1)} %get-tuple-element.16.rmix_ref, bf16[32,128,128]{2,1,0:T(8,128)(2,1)S(1)} %get-tuple-element.17.rkv_ref), custom_call_target="tpu_custom_call" | custom-call | tf_op jit(solution)/shard_map/unpack/pallas_call | solution.py:467
  (10 shorter events, 0.0 us)
Async XLA Ops:
  0.6 1.0 copy-start.4
  1.7 1.0 copy-start.5
  2.7 1.0 copy-start.6
  3.8 1.0 copy-start.7
  4.8 0.7 copy-start.8
  48.3 1.6 copy-start
  49.9 1.0 copy-start.2
  50.9 1.1 copy-start.10
  50.9 1.1 copy-start.9
  128.3 1.9 copy-start.1
  130.2 1.2 copy-start.3

commit v2 on v1

--- a/solution.py
+++ b/solution.py
@@ -5,42 +5,100 @@
 from jax.experimental import pallas as pl
 from jax.experimental.pallas import tpu as pltpu
 
-H, HD, SAMPLES = 32, 64, 8
-TQ, TK, ALIGN = 512, 512, 128
+HD, SAMPLES = 64, 8
+LANES = 2 * HD
+MESH = pl.DeviceIdType.MESH
+TQ, TK, BLOCK, ALIGN = 512, 256, 512, 128
+LEVELS = (8, 2, 1)
 PENALTY = -float(2**20)
-
-
-def attention_kernel(starts, counts, qc_ref, kv_ref, qid_ref, kid_ref, mix_ref, dkv_ref,
-                     kaug, kvx, kvT, acc, pbuf, mbuf):
+SAFE_POWER = 100.0
+
+
+def looped(count, step, state):
+    done = 0
+    for level in LEVELS:
+
+        def several(turn, state, level=level, done=done):
+            for i in range(level):
+                state = step(done + turn * level + i, state)
+            return state
+
+        turns = (count - done) // level
+        state = lax.fori_loop(0, turns, several, state)
+        done = done + turns * level
+    return state
+
+
+def attention_kernel(planes, qc_ref, kv_ref, ids_ref, mix_ref, dkv_ref,
+                     kid, kaug, kvx, kvT, acc, pbuf, mbuf, edges):
+    f32, bf16, i32 = jnp.float32, jnp.bfloat16, jnp.int32
     rows, ext = qc_ref.shape[0], kv_ref.shape[0]
+    _, owners, tok = ids_ref.shape
+    per_block = BLOCK // tok
     factor = 1.0 / math.sqrt(HD)
     log2_factor = factor * math.log2(math.e)
-    f32, bf16 = jnp.float32, jnp.bfloat16
-
-    def one_hot(ids_row, width):
-        sample = lax.broadcasted_iota(jnp.int32, (SAMPLES, width), 0)
+    plane = lax.axis_index("outer")
+
+    before = jnp.where(plane == 0, -1, ids_ref[0])
+    after = jnp.where(plane == planes - 1, SAMPLES, ids_ref[2])
+    parts = (before, ids_ref[1], after)
+    for sample in range(SAMPLES + 1):
+        low = sum((part < sample).astype(i32) for part in parts)
+        edges[sample] = jnp.sum(low)
+    for place, part in enumerate(parts):
+        for owner in range(owners):
+            at = place * owners + owner
+            kid[at // per_block, :, (at % per_block) * tok:(at % per_block + 1) * tok] = part[owner:owner + 1]
+
+    def span(begin, end):
+        first, last = edges[0] * 0, edges[0] * 0 + ext
+        for sample in range(SAMPLES + 1):
+            edge = edges[sample]
+            first = jnp.where(edge <= begin, jnp.maximum(first, edge), first)
+            last = jnp.where(edge >= end, jnp.minimum(last, edge), last)
+        return first, last
+
+    def one_hot(ids_row):
+        width = ids_row.shape[1]
+        sample = lax.broadcasted_iota(i32, (SAMPLES, width), 0)
         return sample == jnp.broadcast_to(ids_row, (SAMPLES, width))
 
-    def prepare(block, _):
-        at = pl.multiple_of(block * TK, TK)
-        here = pl.ds(at, TK)
+    lane = lax.broadcasted_iota(i32, (BLOCK, LANES), 1)
+
+    def clear(block, _):
+        acc[pl.ds(pl.multiple_of(block * BLOCK, BLOCK), BLOCK), :] = jnp.zeros((BLOCK, LANES), f32)
+        return 0
+
+    lax.fori_loop(0, acc.shape[0] // BLOCK, clear, 0)
+
+    def squared(turned):
+        wide = turned.astype(f32)
+        return jnp.sum(wide * wide, axis=0, keepdims=True)
+
+    def prepare(block, largest):
+        here = pl.ds(pl.multiple_of(block * BLOCK, BLOCK), BLOCK)
         tile = kv_ref[here, :]
         turned = tile.T
         kvx[here, :] = tile
         kvT[:, here] = turned
-        penalty = jnp.where(one_hot(kid_ref[:, here], TK), 0.0, PENALTY)
-        penalty = jnp.concatenate([penalty, jnp.zeros((HD - SAMPLES, TK), f32)], axis=0)
+        penalty = jnp.where(one_hot(kid[block]), 0.0, PENALTY)
+        penalty = jnp.concatenate([penalty, jnp.zeros((HD - SAMPLES, BLOCK), f32)], axis=0)
         kaug[here, :] = jnp.concatenate([turned[:HD], penalty.astype(bf16)], axis=0).T
-        acc[here, :] = jnp.zeros((TK, 2 * HD), f32)
-        return 0
-
-    lax.fori_loop(0, ext // TK, prepare, 0)
-    pad = pl.ds(ext, TK)
-    lane = lax.broadcasted_iota(jnp.int32, (TK, 2 * HD), 1)
-    kvx[pad, :] = jnp.zeros((TK, 2 * HD), bf16)
-    kvT[:, pad] = jnp.zeros((2 * HD, TK), bf16)
-    kaug[pad, :] = jnp.where((lane >= HD) & (lane < HD + SAMPLES), PENALTY, 0.0).astype(bf16)
-    acc[pad, :] = jnp.zeros((TK, 2 * HD), f32)
+        return jnp.maximum(largest, squared(turned[:HD]))
+
+    reach_first, reach_last = span(rows, 2 * rows)
+    first_block = reach_first // BLOCK
+    last_block = (reach_last + BLOCK - 1) // BLOCK
+    key_square = lax.fori_loop(first_block, last_block, prepare, jnp.zeros((1, BLOCK), f32))
+    key_most = jnp.max(key_square)
+
+    def pad(block):
+        here = pl.ds(pl.multiple_of(block * BLOCK, BLOCK), BLOCK)
+        kvx[here, :] = jnp.zeros((BLOCK, LANES), bf16)
+        kvT[:, here] = jnp.zeros((LANES, BLOCK), bf16)
+        kaug[here, :] = jnp.where((lane >= HD) & (lane < HD + SAMPLES), PENALTY, 0.0).astype(bf16)
+
+    pad(last_block)
 
     def query_tile(tile, _):
         q_at = pl.multiple_of(tile * TQ, TQ)
@@ -48,16 +106,19 @@
         qc = qc_ref[mine, :]
         qcT = qc.T
         qT, cT = qcT[:HD], qcT[HD:]
-        hot = jnp.where(one_hot(qid_ref[:, mine], TQ), 1.0, 0.0)
+        own = [kid[(rows + q_at) // BLOCK + i] for i in range(TQ // BLOCK)]
+        own = own[0] if len(own) == 1 else jnp.concatenate(own, axis=1)
+        hot = jnp.where(one_hot(own), 1.0, 0.0)
         hot = jnp.concatenate([hot, jnp.zeros((HD - SAMPLES, TQ), f32)], axis=0).astype(bf16)
         q_side = jnp.concatenate([qT, hot], axis=0)
         c_side = jnp.concatenate([jnp.zeros_like(cT), cT], axis=0)
-        lanes = lax.broadcasted_iota(jnp.int32, qc.shape, 1)
+        lanes = lax.broadcasted_iota(i32, qc.shape, 1)
         q_only = jnp.where(lanes < HD, qc, jnp.zeros_like(qc))
         c_only = jnp.where(lanes < HD, jnp.zeros_like(qc), qc)
         cq = jnp.concatenate([c_only, q_only], axis=0)
-        first = starts[tile]
-        count = counts[tile]
+        begin, end = span(rows + q_at, rows + q_at + TQ)
+        first = begin // ALIGN * ALIGN
+        count = (end - first + TK - 1) // TK
 
         def key_rows(step):
             return pl.ds(pl.multiple_of(first + step * TK, ALIGN), TK)
@@ -65,79 +126,96 @@
         def slot(step):
             return pl.ds(pl.multiple_of(step * TK, TK), TK)
 
-        def score_step(step, state):
+        def scores_of(step):
+            return jnp.dot(kaug[key_rows(step), :], q_side, preferred_element_type=f32) * log2_factor
+
+        def bounded_step(step, total):
+            terms = jnp.exp2(scores_of(step))
+            pbuf[slot(step), :] = terms
+            mbuf[step] = jnp.zeros((1, TQ), f32)
+            return total + jnp.sum(terms, axis=0, keepdims=True)
+
+        def running_step(step, state):
             top, total = state
-            scores = jnp.dot(kaug[key_rows(step), :], q_side, preferred_element_type=f32) * log2_factor
+            scores = scores_of(step)
             new_top = jnp.maximum(top, jnp.max(scores, axis=0, keepdims=True))
             terms = jnp.exp2(scores - new_top)
             pbuf[slot(step), :] = terms
             mbuf[step] = new_top
             return new_top, total * jnp.exp2(top - new_top) + jnp.sum(terms, axis=0, keepdims=True)
 
-        top, total = lax.fori_loop(
-            0, count, score_step, (jnp.full((1, TQ), -1e30, f32), jnp.zeros((1, TQ), f32))
-        )
+        def bounded():
+            return jnp.zeros((1, TQ), f32), looped(count, bounded_step, jnp.zeros((1, TQ), f32))
+
+        def running():
+            start = (jnp.full((1, TQ), -1e30, f32), jnp.zeros((1, TQ), f32))
+            return lax.fori_loop(0, count, running_step, start)
+
+        query_most = jnp.max(squared(qT))
+        small = query_most * key_most <= (SAFE_POWER / log2_factor) ** 2
+        top, total = lax.cond(small, bounded, running)
         scale = 1.0 / total
 
+        def weights_of(step):
+            return pbuf[slot(step), :] * (jnp.exp2(mbuf[step] - top) * scale)
+
         def value_step(step, summed):
-            weights = pbuf[slot(step), :] * (jnp.exp2(mbuf[step] - top) * scale)
             return summed + jnp.dot(
-                kvT[HD:, key_rows(step)], weights.astype(bf16), preferred_element_type=f32
+                kvT[HD:, key_rows(step)], weights_of(step).astype(bf16), preferred_element_type=f32
             )
 
-        mixed = lax.fori_loop(0, count, value_step, jnp.zeros((HD, TQ), f32)).astype(bf16)
+        mixed = looped(count, value_step, jnp.zeros((HD, TQ), f32)).astype(bf16)
         row_dot = jnp.sum(cT.astype(f32) * mixed.astype(f32), axis=0, keepdims=True)
 
         def grad_step(step, summed):
             keys = key_rows(step)
-            weights = pbuf[slot(step), :] * (jnp.exp2(mbuf[step] - top) * scale)
+            weights = weights_of(step)
             grad_prob = jnp.dot(kvx[keys, :], c_side, preferred_element_type=f32)
             grad_score = (weights * (grad_prob - row_dot)).astype(bf16)
             pair = jnp.concatenate([weights.astype(bf16), grad_score], axis=1)
             acc[keys, :] += jnp.dot(pair, cq, preferred_element_type=f32)
             return summed + jnp.dot(kvT[:HD, keys], grad_score, preferred_element_type=f32)
 
-        grad_query = lax.fori_loop(0, count, grad_step, jnp.zeros((HD, TQ), f32)) * factor
+        grad_query = looped(count, grad_step, jnp.zeros((HD, TQ), f32)) * factor
         mix_ref[mine, :] = jnp.concatenate([mixed, grad_query.astype(bf16)], axis=0).T
         return 0
 
     lax.fori_loop(0, rows // TQ, query_tile, 0)
 
     def finish(block, _):
-        here = pl.ds(pl.multiple_of(block * TK, TK), TK)
+        here = pl.ds(pl.multiple_of(block * BLOCK, BLOCK), BLOCK)
         grads = acc[here, :]
         dkv_ref[here, :] = jnp.where(lane < HD, grads * factor, grads).astype(bf16)
         return 0
 
-    lax.fori_loop(0, ext // TK, finish, 0)
-
-
-def attention(starts, counts, qc, kv, qid, kid):
+    lax.fori_loop(0, ext // BLOCK, finish, 0)
+
+
+def attention(planes, qc, kv, ids):
     rows, ext = qc.shape[0], kv.shape[0]
     vmem = pl.BlockSpec(memory_space=pltpu.VMEM)
-    smem = pl.BlockSpec(memory_space=pltpu.SMEM)
-    most = 2 * rows + TQ + TK + ALIGN
+    padded = ext + max(TK, BLOCK)
+    steps = (2 * rows + TQ + TK + ALIGN) // TK
+    bf16, f32 = jnp.bfloat16, jnp.float32
     return pl.pallas_call(
-        attention_kernel,
-        out_shape=(jax.ShapeDtypeStruct((rows, 2 * HD), jnp.bfloat16),
-                   jax.ShapeDtypeStruct((ext, 2 * HD), jnp.bfloat16)),
-        in_specs=[smem, smem, vmem, vmem, vmem, vmem],
+        functools.partial(attention_kernel, planes),
+        out_shape=(jax.ShapeDtypeStruct((rows, LANES), bf16),
+                   jax.ShapeDtypeStruct((ext, LANES), bf16)),
+        in_specs=[vmem] * 3,
         out_specs=(vmem, vmem),
         scratch_shapes=[
-            pltpu.VMEM((ext + TK, 2 * HD), jnp.bfloat16),
-            pltpu.VMEM((ext + TK, 2 * HD), jnp.bfloat16),
-            pltpu.VMEM((2 * HD, ext + TK), jnp.bfloat16),
-            pltpu.VMEM((ext + TK, 2 * HD), jnp.float32),
-            pltpu.VMEM(((most + TK - 1) // TK * TK, TQ), jnp.float32),
-            pltpu.VMEM(((most + TK - 1) // TK, 1, TQ), jnp.float32),
+            pltpu.VMEM((ext // BLOCK, 1, BLOCK), jnp.int32),
+            pltpu.VMEM((padded, LANES), bf16),
+            pltpu.VMEM((padded, LANES), bf16),
+            pltpu.VMEM((LANES, padded), bf16),
+            pltpu.VMEM((padded, LANES), f32),
+            pltpu.VMEM((steps * TK, TQ), f32),
+            pltpu.VMEM((steps, 1, TQ), f32),
+            pltpu.SMEM((SAMPLES + 1,), jnp.int32),
         ],
-        compiler_params=pltpu.CompilerParams(vmem_limit_bytes=56 * 2**20),
+        compiler_params=pltpu.CompilerParams(vmem_limit_bytes=60 * 2**20),
         name="attention",
-    )(starts, counts, qc, kv, qid, kid)
-
-
-LANES = 2 * HD
-MESH = pl.DeviceIdType.MESH
+    )(qc, kv, ids)
 
 
 def partner(me, hop, size):
@@ -476,20 +554,8 @@
 
 def on_device(query_rows, key_rows, value_rows, sample_of, cotangent):
     size, planes = lax.axis_size("inner"), lax.axis_size("outer")
-    tok = query_rows.shape[0]
-    rows = tok * size
     qc, kv, ids = collect(size, planes, query_rows, key_rows, value_rows, cotangent, sample_of[None])
-    group = lax.axis_index("outer")
-    before = jnp.where(group == 0, -1, ids[0])
-    after = jnp.where(group == planes - 1, SAMPLES, ids[2])
-    row_ids = ids[1].reshape(rows)
-    ext_ids = jnp.concatenate([before.reshape(rows), row_ids, after.reshape(rows)])
-    tiles = row_ids.reshape(rows // TQ, TQ)
-    low = jnp.sum((ext_ids[None, :] < tiles[:, :1]).astype(jnp.int32), axis=1)
-    high = jnp.sum((ext_ids[None, :] <= tiles[:, -1:]).astype(jnp.int32), axis=1)
-    starts = low // ALIGN * ALIGN
-    counts = (high - starts + TK - 1) // TK
-    mix, dkv = attention(starts, counts, qc, kv, row_ids[None], ext_ids[None])
+    mix, dkv = attention(planes, qc, kv, ids)
     return unpack(*give_back(size, planes, mix, dkv))
 
 

time: 211 us -> 205 us (0.972)
  Pallas kernels: 198 us -> 193 us
    pallas_call x1, Pallas kernels: 76.7 us -> 72.6 us  [give_back(): pl.pallas_call(functools.partial(return_kernel, size, planes), out_shape=...]
    unnamed x24 -> x20, local copies, waits for them, and re-layouts: 10.7 us -> 11.1 us
where the time goes in v2:
time: 205 us; the launch traced here: 204 us
  Pallas kernels  193 us (94%)
  local copies, waits for them, and re-layouts  11.1 us (5%)
    pallas_call x1, Pallas kernels, attention(): pl.pallas_call(functools.partial(attention_kernel, planes), out_shape=(ja...  74.7 us
    pallas_call x1, Pallas kernels, give_back(): pl.pallas_call(functools.partial(return_kernel, size, planes), out_shape=...  72.6 us
    pallas_call x1, Pallas kernels, collect(): pl.pallas_call(functools.partial(collect_kernel, size, planes), out_shape...  42.8 us
    unnamed x20, local copies, waits for them, and re-layouts  11.1 us

profile of v2, /device:TPU:1, one launch (start us, length us, event | category | flops | bytes accessed | tf_op | source)
XLA Modules:
  0.0 204.4 jit_solution(5691631786076224763)
XLA Ops:
  0.6 0.0 copy-start.4
  0.6 1.0 copy-done.4
  1.7 0.0 copy-start.5
  1.7 1.0 copy-done.5
  2.7 0.0 copy-start.6
  2.7 1.0 copy-done.6
  3.8 0.0 copy-start.7
  3.8 1.0 copy-done.7
  4.8 0.0 copy-start.9
  4.8 0.7 copy-done.9
  5.5 42.8 %collect.1 = (bf16[4096,128]{1,0:T(8,128)(2,1)S(1)}, bf16[12288,128]{1,0:T(8,128)(2,1)S(1)}, s32[3,32,128]{2,1,0:T(8,128)S(1)}) custom-call(bf16[128,2048]{1,0:T(8,128)(2,1)S(1)} %copy-done.4, bf16[128,2048]{1,0:T(8,128)(2,1)S(1)} %copy-done.5, bf16[128,2048]{1,0:T(8,128)(2,1)S(1)} %copy-done.6, bf16[128,2048]{1,0:T(8,128)(2,1)S(1)} %copy-done.7, ...), custom_call_target="tpu_custom_call" | custom-call | tf_op jit(solution)/shard_map/collect/pallas_call | solution.py:377
  48.3 0.0 copy-start.1
  48.3 1.6 copy-done.1
  49.9 0.0 copy-start.3
  49.9 1.0 copy-done.3
  50.9 0.0 copy-start.8
  50.9 0.6 copy-done.8
  51.5 74.7 %attention.1 = (bf16[4096,128]{1,0:T(8,128)(2,1)}, bf16[12288,128]{1,0:T(8,128)(2,1)}) custom-call(bf16[4096,128]{1,0:T(8,128)(2,1)} %copy-done.3, bf16[12288,128]{1,0:T(8,128)(2,1)} %copy-done.1, s32[3,32,128]{2,1,0:T(8,128)} %copy-done.8), custom_call_target="tpu_custom_call" | custom-call | tf_op jit(solution)/shard_map/attention/pallas_call | solution.py:200
  126.2 0.0 copy-start
  126.2 1.9 copy-done
  128.1 0.0 copy-start.2
  128.1 1.2 copy-done.2
  129.3 72.6 %give_back.1 = (bf16[32,128,128]{2,1,0:T(8,128)(2,1)S(1)}, bf16[32,128,128]{2,1,0:T(8,128)(2,1)S(1)}) custom-call(bf16[4096,128]{1,0:T(8,128)(2,1)S(1)} %copy-done.2, bf16[12288,128]{1,0:T(8,128)(2,1)S(1)} %copy-done), custom_call_target="tpu_custom_call" | custom-call | tf_op jit(solution)/shard_map/give_back/pallas_call | solution.py:517
  201.9 2.5 %unpack.1 = (bf16[128,2048]{1,0:T(8,128)(2,1)}, bf16[128,2048]{1,0:T(8,128)(2,1)}, bf16[128,2048]{1,0:T(8,128)(2,1)}, bf16[128,2048]{1,0:T(8,128)(2,1)}) custom-call(bf16[32,128,128]{2,1,0:T(8,128)(2,1)S(1)} %get-tuple-element.16.rmix_ref, bf16[32,128,128]{2,1,0:T(8,128)(2,1)S(1)} %get-tuple-element.17.rkv_ref), custom_call_target="tpu_custom_call" | custom-call | tf_op jit(solution)/shard_map/unpack/pallas_call | solution.py:545
Async XLA Ops:
  0.6 1.0 copy-start.4
  1.7 1.0 copy-start.5
  2.7 1.0 copy-start.6
  3.8 1.0 copy-start.7
  4.8 0.7 copy-start.9
  48.3 1.6 copy-start.1
  49.9 1.0 copy-start.3
  50.9 0.6 copy-start.8
  126.2 1.9 copy-start
  128.1 1.2 copy-start.2

commit v3 on v2

--- a/solution.py
+++ b/solution.py
@@ -29,10 +29,15 @@
     return state
 
 
-def attention_kernel(planes, qc_ref, kv_ref, ids_ref, mix_ref, dkv_ref,
-                     kid, kaug, kvx, kvT, acc, pbuf, mbuf, edges):
+def attention_kernel(planes, qc_hbm, kv_hbm, ids_ref, mix_hbm, dkv_hbm,
+                     qc_ref, mix_ref, dkv_ref, kid, kaug, kvx, kvT, acc, pbuf, mbuf, edges,
+                     in_sem, mix_sem, dkv_sem):
     f32, bf16, i32 = jnp.float32, jnp.bfloat16, jnp.int32
-    rows, ext = qc_ref.shape[0], kv_ref.shape[0]
+    rows, ext = qc_hbm.shape[0], kv_hbm.shape[0]
+    kv_in = pltpu.make_async_copy(kv_hbm, kvx.at[pl.ds(0, ext)], in_sem.at[0])
+    qc_in = pltpu.make_async_copy(qc_hbm, qc_ref, in_sem.at[1])
+    kv_in.start()
+    qc_in.start()
     _, owners, tok = ids_ref.shape
     per_block = BLOCK // tok
     factor = 1.0 / math.sqrt(HD)
@@ -77,15 +82,14 @@
 
     def prepare(block, largest):
         here = pl.ds(pl.multiple_of(block * BLOCK, BLOCK), BLOCK)
-        tile = kv_ref[here, :]
-        turned = tile.T
-        kvx[here, :] = tile
+        turned = kvx[here, :].T
         kvT[:, here] = turned
         penalty = jnp.where(one_hot(kid[block]), 0.0, PENALTY)
         penalty = jnp.concatenate([penalty, jnp.zeros((HD - SAMPLES, BLOCK), f32)], axis=0)
         kaug[here, :] = jnp.concatenate([turned[:HD], penalty.astype(bf16)], axis=0).T
         return jnp.maximum(largest, squared(turned[:HD]))
 
+    kv_in.wait()
     reach_first, reach_last = span(rows, 2 * rows)
     first_block = reach_first // BLOCK
     last_block = (reach_last + BLOCK - 1) // BLOCK
@@ -99,6 +103,15 @@
         kaug[here, :] = jnp.where((lane >= HD) & (lane < HD + SAMPLES), PENALTY, 0.0).astype(bf16)
 
     pad(last_block)
+    qc_in.wait()
+
+    def mix_out(tile):
+        mine = pl.ds(pl.multiple_of(tile * TQ, TQ), TQ)
+        return pltpu.make_async_copy(mix_ref.at[mine], mix_hbm.at[mine], mix_sem.at[tile])
+
+    def dkv_out(block):
+        here = pl.ds(pl.multiple_of(block * BLOCK, BLOCK), BLOCK)
+        return pltpu.make_async_copy(dkv_ref.at[here], dkv_hbm.at[here], dkv_sem.at[block])
 
     def query_tile(tile, _):
         q_at = pl.multiple_of(tile * TQ, TQ)
@@ -178,6 +191,7 @@
 
         grad_query = looped(count, grad_step, jnp.zeros((HD, TQ), f32)) * factor
         mix_ref[mine, :] = jnp.concatenate([mixed, grad_query.astype(bf16)], axis=0).T
+        mix_out(tile).start()
         return 0
 
     lax.fori_loop(0, rows // TQ, query_tile, 0)
@@ -186,14 +200,27 @@
         here = pl.ds(pl.multiple_of(block * BLOCK, BLOCK), BLOCK)
         grads = acc[here, :]
         dkv_ref[here, :] = jnp.where(lane < HD, grads * factor, grads).astype(bf16)
+        dkv_out(block).start()
         return 0
 
     lax.fori_loop(0, ext // BLOCK, finish, 0)
+
+    def settle_mix(tile, _):
+        mix_out(tile).wait()
+        return 0
+
+    def settle_dkv(block, _):
+        dkv_out(block).wait()
+        return 0
+
+    lax.fori_loop(0, rows // TQ, settle_mix, 0)
+    lax.fori_loop(0, ext // BLOCK, settle_dkv, 0)
 
 
 def attention(planes, qc, kv, ids):
     rows, ext = qc.shape[0], kv.shape[0]
     vmem = pl.BlockSpec(memory_space=pltpu.VMEM)
+    hbm = pl.BlockSpec(memory_space=pl.ANY)
     padded = ext + max(TK, BLOCK)
     steps = (2 * rows + TQ + TK + ALIGN) // TK
     bf16, f32 = jnp.bfloat16, jnp.float32
@@ -201,9 +228,12 @@
         functools.partial(attention_kernel, planes),
         out_shape=(jax.ShapeDtypeStruct((rows, LANES), bf16),
                    jax.ShapeDtypeStruct((ext, LANES), bf16)),
-        in_specs=[vmem] * 3,
-        out_specs=(vmem, vmem),
+        in_specs=[hbm, hbm, vmem],
+        out_specs=(hbm, hbm),
         scratch_shapes=[
+            pltpu.VMEM((rows, LANES), bf16),
+            pltpu.VMEM((rows, LANES), bf16),
+            pltpu.VMEM((ext, LANES), bf16),
             pltpu.VMEM((ext // BLOCK, 1, BLOCK), jnp.int32),
             pltpu.VMEM((padded, LANES), bf16),
             pltpu.VMEM((padded, LANES), bf16),
@@ -212,6 +242,9 @@
             pltpu.VMEM((steps * TK, TQ), f32),
             pltpu.VMEM((steps, 1, TQ), f32),
             pltpu.SMEM((SAMPLES + 1,), jnp.int32),
+            pltpu.SemaphoreType.DMA((2,)),
+            pltpu.SemaphoreType.DMA((rows // TQ,)),
+            pltpu.SemaphoreType.DMA((ext // BLOCK,)),
         ],
         compiler_params=pltpu.CompilerParams(vmem_limit_bytes=60 * 2**20),
         name="attention",
@@ -222,33 +255,64 @@
     return lax.rem(me + hop, size)
 
 
+def hops():
+    found = []
+    for start in ((1, 2), (1, 1), (0, 1), (2, 2), (0, 2)):
+        turned = []
+        dx, dy = start
+        for _ in range(4):
+            if (dx % SIDE, dy % SIDE) not in turned:
+                turned.append((dx % SIDE, dy % SIDE))
+            dx, dy = -dy, dx
+        found += [(x, y, core) for core in range(2) for x, y in turned]
+    return found + [(0, 0, 1)]
+
+
+SIDE = 4
+HOPS = hops()
+
+
+def moved(me, hop, sign=1):
+    x, y, core = me // (2 * SIDE), lax.rem(me // 2, SIDE), lax.rem(me, 2)
+    dx, dy, dcore = hop
+    x = lax.rem(x + (dx if sign > 0 else SIDE - dx), SIDE)
+    y = lax.rem(y + (dy if sign > 0 else SIDE - dy), SIDE)
+    return (x * SIDE + y) * 2 + lax.rem(core + dcore, 2)
+
+
+def greet_all(me, above, below):
+    barrier = pltpu.get_barrier_semaphore()
+    for hop in HOPS:
+        pl.semaphore_signal(barrier, inc=1, device_id={"inner": moved(me, hop)}, device_id_type=MESH)
+    for other in (above, below):
+        pl.semaphore_signal(barrier, inc=1, device_id={"outer": other}, device_id_type=MESH)
+    return barrier, len(HOPS) + 2
+
+
 def packed(first, second, head):
     columns = slice(head * HD, (head + 1) * HD)
     return jnp.concatenate([first[:, columns], second[:, columns]], axis=1)
 
 
-def collect_kernel(size, planes, q_ref, k_ref, v_ref, c_ref, id_ref, qc_ref, kv_ref, ids_ref,
-                   qc_pack, kv_pack, own_sem, kv_send, kv_recv, qc_send, qc_recv,
+def collect_kernel(size, planes, q_hbm, k_hbm, v_hbm, c_hbm, id_ref, qc_ref, kv_ref, ids_ref,
+                   q_ref, k_ref, v_ref, c_ref, qc_pack, kv_pack, in_sem, own_sem, kv_send, kv_recv, qc_send, qc_recv,
                    id_send, id_recv, z_send, z_recv, zid_send, zid_recv):
     me, plane = lax.axis_index("inner"), lax.axis_index("outer")
     tok = q_ref.shape[0]
     rows = tok * size
-    chunks = z_send.shape[1]
-    share = size // chunks
     above, below = partner(plane, 1, planes), partner(plane, planes - 1, planes)
-
-    barrier = pltpu.get_barrier_semaphore()
-
-    def greet(hop, _):
-        pl.semaphore_signal(barrier, inc=1, device_id={"inner": partner(me, hop, size)}, device_id_type=MESH)
-        return 0
-
-    lax.fori_loop(1, size, greet, 0)
-    for other in (above, below):
-        pl.semaphore_signal(barrier, inc=1, device_id={"outer": other}, device_id_type=MESH)
+    loads = [
+        pltpu.make_async_copy(source, target, in_sem.at[i])
+        for i, (source, target) in enumerate(((k_hbm, k_ref), (v_hbm, v_ref), (q_hbm, q_ref), (c_hbm, c_ref)))
+    ]
+    for load in loads:
+        load.start()
+    barrier, greeted = greet_all(me, above, below)
+    loads[0].wait()
+    loads[1].wait()
     for head in range(size):
         kv_pack[head] = packed(k_ref, v_ref, head)
-    pl.semaphore_wait(barrier, size + 1)
+    pl.semaphore_wait(barrier, greeted)
 
     def block(owner, base=0):
         return pl.ds(pl.multiple_of(base + owner * tok, tok), tok)
@@ -271,71 +335,46 @@
             send_sem=id_send.at[other], recv_sem=id_recv.at[slot],
             device_id={"inner": other}, device_id_type=MESH)
 
+    def z_copies(slot):
+        src = kv_ref.at[block(slot, rows)]
+        up = pltpu.make_async_remote_copy(
+            src_ref=src, dst_ref=kv_ref.at[block(slot)],
+            send_sem=z_send.at[0, slot], recv_sem=z_recv.at[0, slot],
+            device_id={"outer": above}, device_id_type=MESH)
+        down = pltpu.make_async_remote_copy(
+            src_ref=src, dst_ref=kv_ref.at[block(slot, 2 * rows)],
+            send_sem=z_send.at[1, slot], recv_sem=z_recv.at[1, slot],
+            device_id={"outer": below}, device_id_type=MESH)
+        return up, down
+
     own_kv = pltpu.make_async_copy(kv_pack.at[me], kv_ref.at[block(me, rows)], own_sem.at[0])
     own_id = pltpu.make_async_copy(id_ref, ids_ref.at[1, pl.ds(me, 1)], own_sem.at[1])
     own_kv.start()
     own_id.start()
-
-    def send_kv(hop, _):
-        other = partner(me, hop, size)
+    for hop in HOPS:
+        other = moved(me, hop)
         kv_copy(other, me).start()
         id_copy(other, me).start()
-        return 0
-
-    lax.fori_loop(1, size, send_kv, 0)
+    own_kv.wait()
+    for copy in z_copies(me):
+        copy.start()
+    loads[2].wait()
+    loads[3].wait()
     for head in range(size):
         qc_pack[head] = packed(q_ref, c_ref, head)
     own_qc = pltpu.make_async_copy(qc_pack.at[me], qc_ref.at[block(me)], own_sem.at[2])
     own_qc.start()
-
-    def send_qc(hop, _):
-        qc_copy(partner(me, hop, size), me).start()
-        return 0
-
-    lax.fori_loop(1, size, send_qc, 0)
-
-    own_kv.wait()
+    for hop in HOPS:
+        qc_copy(moved(me, hop), me).start()
+    for hop in HOPS:
+        slot = moved(me, hop, -1)
+        kv_copy(slot, slot).wait_recv()
+        for copy in z_copies(slot):
+            copy.start()
     own_id.wait()
-
-    def z_copies(chunk):
-        src = kv_ref.at[pl.ds(pl.multiple_of(rows + chunk * (share * tok), share * tok), share * tok)]
-        up = pltpu.make_async_remote_copy(
-            src_ref=src, dst_ref=kv_ref.at[pl.ds(pl.multiple_of(chunk * (share * tok), share * tok), share * tok)],
-            send_sem=z_send.at[0, chunk], recv_sem=z_recv.at[0, chunk],
-            device_id={"outer": above}, device_id_type=MESH)
-        down = pltpu.make_async_remote_copy(
-            src_ref=src, dst_ref=kv_ref.at[pl.ds(pl.multiple_of(2 * rows + chunk * (share * tok), share * tok), share * tok)],
-            send_sem=z_send.at[1, chunk], recv_sem=z_recv.at[1, chunk],
-            device_id={"outer": below}, device_id_type=MESH)
-        return up, down
-
-    home = me // share
-
-    def pass_on(step, _):
-        chunk = lax.rem(home + chunks - step, chunks)
-
-        def arrive(i, _):
-            slot = chunk * share + i
-
-            @pl.when(slot != me)
-            def _():
-                kv_copy(slot, slot).wait_recv()
-
-            return 0
-
-        lax.fori_loop(0, share, arrive, 0)
-        for copy in z_copies(chunk):
-            copy.start()
-        return 0
-
-    lax.fori_loop(0, chunks, pass_on, 0)
-
-    def id_arrive(hop, _):
-        slot = partner(me, hop, size)
+    for hop in HOPS:
+        slot = moved(me, hop, -1)
         id_copy(slot, slot).wait_recv()
-        return 0
-
-    lax.fori_loop(1, size, id_arrive, 0)
     id_up = pltpu.make_async_remote_copy(
         src_ref=ids_ref.at[1], dst_ref=ids_ref.at[0], send_sem=zid_send.at[0], recv_sem=zid_recv.at[0],
         device_id={"outer": above}, device_id_type=MESH)
@@ -344,7 +383,6 @@
         device_id={"outer": below}, device_id_type=MESH)
     id_up.start()
     id_down.start()
-
     own_qc.wait()
 
     def settle(hop, _):
@@ -359,73 +397,60 @@
     id_up.wait()
     id_down.wait()
 
-    def settle_z(chunk, _):
-        for copy in z_copies(chunk):
+    def settle_z(slot, _):
+        for copy in z_copies(slot):
             copy.wait()
         return 0
 
-    lax.fori_loop(0, chunks, settle_z, 0)
+    lax.fori_loop(0, size, settle_z, 0)
 
 
 def collect(size, planes, q, k, v, c, ids):
-    tok = q.shape[0]
+    tok, width = q.shape
     rows = tok * size
     vmem = pl.BlockSpec(memory_space=pltpu.VMEM)
     hbm = pl.BlockSpec(memory_space=pl.ANY)
     dma = pltpu.SemaphoreType.DMA
-    chunks = 8
     return pl.pallas_call(
         functools.partial(collect_kernel, size, planes),
         out_shape=(jax.ShapeDtypeStruct((rows, LANES), jnp.bfloat16),
                    jax.ShapeDtypeStruct((3 * rows, LANES), jnp.bfloat16),
                    jax.ShapeDtypeStruct((3, size, tok), jnp.int32)),
-        in_specs=[vmem] * 5,
+        in_specs=[hbm] * 4 + [vmem],
         out_specs=(hbm, hbm, vmem),
-        scratch_shapes=[
+        scratch_shapes=[pltpu.VMEM((tok, width), jnp.bfloat16)] * 4 + [
             pltpu.VMEM((size, tok, LANES), jnp.bfloat16),
             pltpu.VMEM((size, tok, LANES), jnp.bfloat16),
-            dma((3,)), dma((size,)), dma((size,)), dma((size,)), dma((size,)),
-            dma((size,)), dma((size,)), dma((2, chunks)), dma((2, chunks)), dma((2,)), dma((2,)),
+            dma((4,)), dma((3,)), dma((size,)), dma((size,)), dma((size,)), dma((size,)),
+            dma((size,)), dma((size,)), dma((2, size)), dma((2, size)), dma((2,)), dma((2,)),
         ],
-        compiler_params=pltpu.CompilerParams(collective_id=0, has_side_effects=True, vmem_limit_bytes=32 * 2**20),
+        compiler_params=pltpu.CompilerParams(collective_id=0, has_side_effects=True, vmem_limit_bytes=60 * 2**20),
         name="collect",
     )(q, k, v, c, ids)
 
 
-def return_kernel(size, planes, mix_ref, dkv_ref, rmix_ref, rkv_ref, from_z, total,
+def return_kernel(size, planes, mix_ref, dkv_ref, rmix_ref, rkv_ref, from_z, own, total,
                   own_sem, mix_send, mix_recv, kv_send, kv_recv, z_send, z_recv):
     me, plane = lax.axis_index("inner"), lax.axis_index("outer")
     rows = mix_ref.shape[0]
     tok = rows // size
-    chunks = z_send.shape[1]
-    share = size // chunks
-    step_rows = share * tok
     above, below = partner(plane, 1, planes), partner(plane, planes - 1, planes)
-    barrier = pltpu.get_barrier_semaphore()
-
-    def greet(hop, _):
-        pl.semaphore_signal(barrier, inc=1, device_id={"inner": partner(me, hop, size)}, device_id_type=MESH)
-        return 0
-
-    lax.fori_loop(1, size, greet, 0)
-    for other in (above, below):
-        pl.semaphore_signal(barrier, inc=1, device_id={"outer": other}, device_id_type=MESH)
-    pl.semaphore_wait(barrier, size + 1)
-
-    def block(owner):
-        return pl.ds(pl.multiple_of(owner * tok, tok), tok)
-
-    def part(chunk, base=0):
-        return pl.ds(pl.multiple_of(base + chunk * step_rows, step_rows), step_rows)
-
-    def z_copies(chunk):
+    own_in = pltpu.make_async_copy(dkv_ref.at[pl.ds(rows, rows)], own, own_sem.at[2])
+    own_in.start()
+    barrier, greeted = greet_all(me, above, below)
+    pl.semaphore_wait(barrier, greeted)
+
+    def block(owner, base=0):
+        return pl.ds(pl.multiple_of(base + owner * tok, tok), tok)
+
+    def z_copies(slot):
         down = pltpu.make_async_remote_copy(
-            src_ref=dkv_ref.at[part(chunk)], dst_ref=from_z.at[0, part(chunk)],
-            send_sem=z_send.at[0, chunk], recv_sem=z_recv.at[0, chunk],
+            src_ref=dkv_ref.at[block(slot)], dst_ref=from_z.at[0, block(slot)],
+            send_sem=z_send.at[0, slot], recv_sem=z_recv.at[0, slot],
             device_id={"outer": below}, device_id_type=MESH)
         up = pltpu.make_async_remote_copy(
-            src_ref=dkv_ref.at[part(chunk, 2 * rows)], dst_ref=from_z.at[1, part(chunk)],
-            send_sem=z_send.at[1, chunk], recv_sem=z_recv.at[1, chunk],
+            src_ref=dkv_ref.at[block(slot, 2 * rows)], dst_ref=from_z.at[1, block(slot)],
+            send_sem=z_send.at[1, slot], recv_sem=z_recv.at[1, slot],
             device_id={"outer": above}, device_id_type=MESH)
         return down, up
 
@@ -441,50 +466,33 @@
             send_sem=kv_send.at[other], recv_sem=kv_recv.at[slot],
             device_id={"inner": other}, device_id_type=MESH)
 
-    home = me // share
-
-    def send_z(step, _):
-        for copy in z_copies(lax.rem(home + step, chunks)):
+    for hop in HOPS:
+        other = moved(me, hop)
+        for copy in z_copies(other):
             copy.start()
-        return 0
-
-    lax.fori_loop(0, chunks, send_z, 0)
+        mix_copy(other, me).start()
+    for copy in z_copies(me):
+        copy.start()
     own_mix = pltpu.make_async_copy(mix_ref.at[block(me)], rmix_ref.at[me], own_sem.at[0])
     own_mix.start()
-
-    def send_mix(hop, _):
-        mix_copy(partner(me, hop, size), me).start()
-        return 0
-
-    lax.fori_loop(1, size, send_mix, 0)
     own_kv = pltpu.make_async_copy(total.at[block(me)], rkv_ref.at[me], own_sem.at[1])
-
-    def add_up(step, _):
-        chunk = lax.rem(home + step, chunks)
-        for copy in z_copies(chunk):
+    own_in.wait()
+
+    def add_up(other):
+        for copy in z_copies(other):
             copy.wait_recv()
-        mine = dkv_ref[part(chunk, rows), :].astype(jnp.float32)
-        first = from_z[0, part(chunk), :].astype(jnp.float32)
-        second = from_z[1, part(chunk), :].astype(jnp.float32)
-        total[part(chunk), :] = (mine + first + second).astype(jnp.bfloat16)
-
-        def send(i, _):
-            other = chunk * share + i
-
-            @pl.when(other != me)
-            def _():
-                kv_copy(other, me).start()
-
-            @pl.when(other == me)
-            def _():
-                own_kv.start()
-
-            return 0
-
-        lax.fori_loop(0, share, send, 0)
-        return 0
-
-    lax.fori_loop(0, chunks, add_up, 0)
+        here = block(other)
+        mine = own[here, :].astype(jnp.float32)
+        first = from_z[0, here, :].astype(jnp.float32)
+        second = from_z[1, here, :].astype(jnp.float32)
+        total[here, :] = (mine + first + second).astype(jnp.bfloat16)
+
+    for hop in HOPS:
+        other = moved(me, hop)
+        add_up(other)
+        kv_copy(other, me).start()
+    add_up(me)
+    own_kv.start()
     own_mix.wait()
     own_kv.wait()
 
@@ -498,33 +506,32 @@
 
     lax.fori_loop(1, size, settle, 0)
 
-    def settle_z(chunk, _):
-        for copy in z_copies(chunk):
+    def settle_z(slot, _):
+        for copy in z_copies(slot):
             copy.wait_send()
         return 0
 
-    lax.fori_loop(0, chunks, settle_z, 0)
+    lax.fori_loop(0, size, settle_z, 0)
 
 
 def give_back(size, planes, mix, dkv):
     rows = mix.shape[0]
     tok = rows // size
-    vmem = pl.BlockSpec(memory_space=pltpu.VMEM)
     hbm = pl.BlockSpec(memory_space=pl.ANY)
     dma = pltpu.SemaphoreType.DMA
-    chunks = 8
     got = jax.ShapeDtypeStruct((size, tok, LANES), jnp.bfloat16)
     return pl.pallas_call(
         functools.partial(return_kernel, size, planes),
         out_shape=(got, got),
-        in_specs=[vmem, vmem],
+        in_specs=[hbm, hbm],
         out_specs=(hbm, hbm),
         scratch_shapes=[
             pltpu.VMEM((2, rows, LANES), jnp.bfloat16),
             pltpu.VMEM((rows, LANES), jnp.bfloat16),
-            dma((2,)), dma((size,)), dma((size,)), dma((size,)), dma((size,)), dma((2, chunks)), dma((2, chunks)),
+            pltpu.VMEM((rows, LANES), jnp.bfloat16),
+            dma((3,)), dma((size,)), dma((size,)), dma((size,)), dma((size,)), dma((2, size)), dma((2, size)),
         ],
-        compiler_params=pltpu.CompilerParams(collective_id=1, has_side_effects=True, vmem_limit_bytes=32 * 2**20),
+        compiler_params=pltpu.CompilerParams(collective_id=1, has_side_effects=True, vmem_limit_bytes=60 * 2**20),
         name="give_back",
     )(mix, dkv)
 

time: 205 us -> 175 us (0.85)
  Pallas kernels: 193 us -> 171 us
  local copies, waits for them, and re-layouts: 11.1 us -> 2.44 us
    pallas_call x1, Pallas kernels: 74.7 us -> 57.3 us  [attention(): pl.pallas_call(functools.partial(attention_kernel, planes), out_shape=(ja...]
    unnamed x20 -> x4, local copies, waits for them, and re-layouts: 11.1 us -> 2.44 us
    pallas_call x1, Pallas kernels: 72.6 us -> 67.6 us  [give_back(): pl.pallas_call(functools.partial(return_kernel, size, planes), out_shape=...]
where the time goes in v3:
time: 175 us; the launch traced here: 174 us
  Pallas kernels  171 us (98%)
  local copies, waits for them, and re-layouts  2.44 us (1%)
    pallas_call x1, Pallas kernels, give_back(): pl.pallas_call(functools.partial(return_kernel, size, planes), out_shape=...  67.6 us
    pallas_call x1, Pallas kernels, attention(): pl.pallas_call(functools.partial(attention_kernel, planes), out_shape=(ja...  57.3 us
    pallas_call x1, Pallas kernels, collect(): pl.pallas_call(functools.partial(collect_kernel, size, planes), out_shape...  43.7 us

profile of v3, /device:TPU:1, one launch (start us, length us, event | category | flops | bytes accessed | tf_op | source)
XLA Modules:
  0.0 174.3 jit_solution(5387564972840207679)
XLA Ops:
  0.6 43.7 %collect.1 = (bf16[4096,128]{1,0:T(8,128)(2,1)}, bf16[12288,128]{1,0:T(8,128)(2,1)}, s32[3,32,128]{2,1,0:T(8,128)}) custom-call(bf16[128,2048]{1,0:T(8,128)(2,1)} %q_hbm.1, bf16[128,2048]{1,0:T(8,128)(2,1)} %k_hbm.1, bf16[128,2048]{1,0:T(8,128)(2,1)} %v_hbm.1, bf16[128,2048]{1,0:T(8,128)(2,1)} %c_hbm.1, s32[1,128]{1,0:T(1,128)} %bitcast.1), custom_call_target="tpu_custom_call" | custom-call | tf_op jit(solution)/shard_map/collect/pallas_call | solution.py:414
  44.4 57.3 %attention.1 = (bf16[4096,128]{1,0:T(8,128)(2,1)}, bf16[12288,128]{1,0:T(8,128)(2,1)}) custom-call(bf16[4096,128]{1,0:T(8,128)(2,1)} %get-tuple-element.11.qc_hbm, bf16[12288,128]{1,0:T(8,128)(2,1)} %get-tuple-element.12.kv_hbm, s32[3,32,128]{2,1,0:T(8,128)} %get-tuple-element.13.ids_ref), custom_call_target="tpu_custom_call" | custom-call | tf_op jit(solution)/shard_map/attention/pallas_call | solution.py:227
  101.7 67.6 %give_back.1 = (bf16[32,128,128]{2,1,0:T(8,128)(2,1)}, bf16[32,128,128]{2,1,0:T(8,128)(2,1)}) custom-call(bf16[4096,128]{1,0:T(8,128)(2,1)} %get-tuple-element.14.mix_ref, bf16[12288,128]{1,0:T(8,128)(2,1)} %get-tuple-element.15.dkv_ref), custom_call_target="tpu_custom_call" | custom-call | tf_op jit(solution)/shard_map/give_back/pallas_call | solution.py:523
  169.3 0.0 copy-start
  169.4 1.2 copy-done
  170.6 0.0 copy-start.1
  170.6 1.2 copy-done.1
  171.8 2.5 %unpack.1 = (bf16[128,2048]{1,0:T(8,128)(2,1)}, bf16[128,2048]{1,0:T(8,128)(2,1)}, bf16[128,2048]{1,0:T(8,128)(2,1)}, bf16[128,2048]{1,0:T(8,128)(2,1)}) custom-call(bf16[32,128,128]{2,1,0:T(8,128)(2,1)S(1)} %copy-done, bf16[32,128,128]{2,1,0:T(8,128)(2,1)S(1)} %copy-done.1), custom_call_target="tpu_custom_call" | custom-call | tf_op jit(solution)/shard_map/unpack/pallas_call | solution.py:552
Async XLA Ops:
  169.3 1.2 copy-start
  170.6 1.2 copy-start.1

commit v4 on v3

--- a/solution.py
+++ b/solution.py
@@ -14,9 +14,9 @@
 SAFE_POWER = 100.0
 
 
-def looped(count, step, state):
+def looped(count, step, state, levels=None):
     done = 0
-    for level in LEVELS:
+    for level in levels or LEVELS:
 
         def several(turn, state, level=level, done=done):
             for i in range(level):
@@ -30,7 +30,7 @@
 
 
 def attention_kernel(planes, qc_hbm, kv_hbm, ids_ref, mix_hbm, dkv_hbm,
-                     qc_ref, mix_ref, dkv_ref, kid, kaug, kvx, kvT, acc, pbuf, mbuf, edges,
+                     qc_ref, kid, kaug, kvx, kvT, acc, pbuf, mbuf, edges,
                      in_sem, mix_sem, dkv_sem):
     f32, bf16, i32 = jnp.float32, jnp.bfloat16, jnp.int32
     rows, ext = qc_hbm.shape[0], kv_hbm.shape[0]
@@ -74,7 +74,7 @@
         acc[pl.ds(pl.multiple_of(block * BLOCK, BLOCK), BLOCK), :] = jnp.zeros((BLOCK, LANES), f32)
         return 0
 
-    lax.fori_loop(0, acc.shape[0] // BLOCK, clear, 0)
+    looped(acc.shape[0] // BLOCK, clear, 0, (5, 1))
 
     def squared(turned):
         wide = turned.astype(f32)
@@ -93,7 +93,9 @@
     reach_first, reach_last = span(rows, 2 * rows)
     first_block = reach_first // BLOCK
     last_block = (reach_last + BLOCK - 1) // BLOCK
-    key_square = lax.fori_loop(first_block, last_block, prepare, jnp.zeros((1, BLOCK), f32))
+    key_square = looped(
+        last_block - first_block, lambda i, largest: prepare(first_block + i, largest), jnp.zeros((1, BLOCK), f32), (4, 1)
+    )
     key_most = jnp.max(key_square)
 
     def pad(block):
@@ -107,11 +109,11 @@
 
     def mix_out(tile):
         mine = pl.ds(pl.multiple_of(tile * TQ, TQ), TQ)
-        return pltpu.make_async_copy(mix_ref.at[mine], mix_hbm.at[mine], mix_sem.at[tile])
+        return pltpu.make_async_copy(qc_ref.at[mine], mix_hbm.at[mine], mix_sem.at[tile])
 
     def dkv_out(block):
         here = pl.ds(pl.multiple_of(block * BLOCK, BLOCK), BLOCK)
-        return pltpu.make_async_copy(dkv_ref.at[here], dkv_hbm.at[here], dkv_sem.at[block])
+        return pltpu.make_async_copy(kvx.at[here], dkv_hbm.at[here], dkv_sem.at[block])
 
     def query_tile(tile, _):
         q_at = pl.multiple_of(tile * TQ, TQ)
@@ -190,7 +192,7 @@
             return summed + jnp.dot(kvT[:HD, keys], grad_score, preferred_element_type=f32)
 
         grad_query = looped(count, grad_step, jnp.zeros((HD, TQ), f32)) * factor
-        mix_ref[mine, :] = jnp.concatenate([mixed, grad_query.astype(bf16)], axis=0).T
+        qc_ref[mine, :] = jnp.concatenate([mixed, grad_query.astype(bf16)], axis=0).T
         mix_out(tile).start()
         return 0
 
@@ -199,11 +201,11 @@
     def finish(block, _):
         here = pl.ds(pl.multiple_of(block * BLOCK, BLOCK), BLOCK)
         grads = acc[here, :]
-        dkv_ref[here, :] = jnp.where(lane < HD, grads * factor, grads).astype(bf16)
+        kvx[here, :] = jnp.where(lane < HD, grads * factor, grads).astype(bf16)
         dkv_out(block).start()
         return 0
 
-    lax.fori_loop(0, ext // BLOCK, finish, 0)
+    looped(ext // BLOCK, finish, 0, (4, 1))
 
     def settle_mix(tile, _):
         mix_out(tile).wait()
@@ -232,8 +234,6 @@
         out_specs=(hbm, hbm),
         scratch_shapes=[
             pltpu.VMEM((rows, LANES), bf16),
-            pltpu.VMEM((rows, LANES), bf16),
-            pltpu.VMEM((ext, LANES), bf16),
             pltpu.VMEM((ext // BLOCK, 1, BLOCK), jnp.int32),
             pltpu.VMEM((padded, LANES), bf16),
             pltpu.VMEM((padded, LANES), bf16),
@@ -536,25 +536,59 @@
     )(mix, dkv)
 
 
-def unpack_kernel(rmix_ref, rkv_ref, att_ref, dq_ref, dk_ref, dv_ref):
-    for head in range(rmix_ref.shape[0]):
-        columns = slice(head * HD, (head + 1) * HD)
-        mix, grads = rmix_ref[head], rkv_ref[head]
-        att_ref[:, columns] = mix[:, :HD]
-        dq_ref[:, columns] = mix[:, HD:]
-        dk_ref[:, columns] = grads[:, :HD]
-        dv_ref[:, columns] = grads[:, HD:]
+def unpack_kernel(rmix_hbm, rkv_hbm, att_hbm, dq_hbm, dk_hbm, dv_hbm, rmix, rkv, att, dq, dk, dv, in_sem, out_sem):
+    heads = rmix.shape[0]
+    groups = in_sem.shape[1]
+    each = heads // groups
+    outs = ((att, att_hbm), (dq, dq_hbm), (dk, dk_hbm), (dv, dv_hbm))
+
+    def loads(group):
+        part = slice(group * each, (group + 1) * each)
+        return [
+            pltpu.make_async_copy(source.at[part], target.at[part], in_sem.at[i, group])
+            for i, (source, target) in enumerate(((rmix_hbm, rmix), (rkv_hbm, rkv)))
+        ]
+
+    def stores(group):
+        columns = slice(group * each * HD, (group + 1) * each * HD)
+        return [
+            pltpu.make_async_copy(source.at[:, columns], target.at[:, columns], out_sem.at[i, group])
+            for i, (source, target) in enumerate(outs)
+        ]
+
+    for group in range(groups):
+        for copy in loads(group):
+            copy.start()
+    for group in range(groups):
+        for copy in loads(group):
+            copy.wait()
+        for head in range(group * each, (group + 1) * each):
+            columns = slice(head * HD, (head + 1) * HD)
+            mix, grads = rmix[head], rkv[head]
+            att[:, columns] = mix[:, :HD]
+            dq[:, columns] = mix[:, HD:]
+            dk[:, columns] = grads[:, :HD]
+            dv[:, columns] = grads[:, HD:]
+        for copy in stores(group):
+            copy.start()
+    for group in range(groups):
+        for copy in stores(group):
+            copy.wait()
 
 
 def unpack(rmix, rkv):
     heads, tok, _ = rmix.shape
-    vmem = pl.BlockSpec(memory_space=pltpu.VMEM)
+    groups = 4
+    hbm = pl.BlockSpec(memory_space=pl.ANY)
+    rows = (tok, heads * HD)
     return pl.pallas_call(
         unpack_kernel,
-        out_shape=(jax.ShapeDtypeStruct((tok, heads * HD), jnp.bfloat16),) * 4,
-        in_specs=[vmem, vmem],
-        out_specs=(vmem,) * 4,
-        compiler_params=pltpu.CompilerParams(vmem_limit_bytes=32 * 2**20),
+        out_shape=(jax.ShapeDtypeStruct(rows, jnp.bfloat16),) * 4,
+        in_specs=[hbm, hbm],
+        out_specs=(hbm,) * 4,
+        scratch_shapes=[pltpu.VMEM(rmix.shape, jnp.bfloat16)] * 2 + [pltpu.VMEM(rows, jnp.bfloat16)] * 4 + [
+            pltpu.SemaphoreType.DMA((2, groups)), pltpu.SemaphoreType.DMA((4, groups))],
+        compiler_params=pltpu.CompilerParams(vmem_limit_bytes=60 * 2**20),
         name="unpack",
     )(rmix, rkv)
 

time: 175 us -> 172 us (0.983)
  local copies, waits for them, and re-layouts: 2.44 us -> 0 us
    pallas_call x1, Pallas kernels: 67.6 us -> 32.7 us  [give_back(): pl.pallas_call(functools.partial(return_kernel, size, planes), out_shape=...]
    pallas_call x1, Pallas kernels: 57.3 us -> 90.6 us  [attention(): pl.pallas_call(functools.partial(attention_kernel, planes), out_shape=(ja...]
    unnamed x4 -> x0, local copies, waits for them, and re-layouts: 2.44 us -> none
where the time goes in v4:
time: 172 us; the launch traced here: 171 us
  Pallas kernels  171 us (99%)
    pallas_call x1, Pallas kernels, attention(): pl.pallas_call(functools.partial(attention_kernel, planes), out_shape=(ja...  90.6 us
    pallas_call x1, Pallas kernels, collect(): pl.pallas_call(functools.partial(collect_kernel, size, planes), out_shape...  43.8 us
    pallas_call x1, Pallas kernels, give_back(): pl.pallas_call(functools.partial(return_kernel, size, planes), out_shape=...  32.7 us
    pallas_call x1, Pallas kernels, unpack(): pl.pallas_call(unpack_kernel, out_shape=(jax.ShapeDtypeStruct(rows, jnp.b...  3.48 us

profile of v4, /device:TPU:1, one launch (start us, length us, event | category | flops | bytes accessed | tf_op | source)
XLA Modules:
  0.0 171.3 jit_solution(13473502524882405309)
XLA Ops:
  0.6 43.8 %collect.1 = (bf16[4096,128]{1,0:T(8,128)(2,1)}, bf16[12288,128]{1,0:T(8,128)(2,1)}, s32[3,32,128]{2,1,0:T(8,128)}) custom-call(bf16[128,2048]{1,0:T(8,128)(2,1)} %q_hbm.1, bf16[128,2048]{1,0:T(8,128)(2,1)} %k_hbm.1, bf16[128,2048]{1,0:T(8,128)(2,1)} %v_hbm.1, bf16[128,2048]{1,0:T(8,128)(2,1)} %c_hbm.1, s32[1,128]{1,0:T(1,128)} %bitcast.1), custom_call_target="tpu_custom_call" | custom-call | tf_op jit(solution)/shard_map/collect/pallas_call | solution.py:414
  44.4 90.6 %attention.1 = (bf16[4096,128]{1,0:T(8,128)(2,1)}, bf16[12288,128]{1,0:T(8,128)(2,1)}) custom-call(bf16[4096,128]{1,0:T(8,128)(2,1)} %get-tuple-element.11.qc_hbm, bf16[12288,128]{1,0:T(8,128)(2,1)} %get-tuple-element.12.kv_hbm, s32[3,32,128]{2,1,0:T(8,128)} %get-tuple-element.13.ids_ref), custom_call_target="tpu_custom_call" | custom-call | tf_op jit(solution)/shard_map/attention/pallas_call | solution.py:229
  135.0 32.7 %give_back.1 = (bf16[32,128,128]{2,1,0:T(8,128)(2,1)}, bf16[32,128,128]{2,1,0:T(8,128)(2,1)}) custom-call(bf16[4096,128]{1,0:T(8,128)(2,1)} %get-tuple-element.14.mix_ref, bf16[12288,128]{1,0:T(8,128)(2,1)} %get-tuple-element.15.dkv_ref), custom_call_target="tpu_custom_call" | custom-call | tf_op jit(solution)/shard_map/give_back/pallas_call | solution.py:523
  167.7 3.5 %unpack.1 = (bf16[128,2048]{1,0:T(8,128)(2,1)}, bf16[128,2048]{1,0:T(8,128)(2,1)}, bf16[128,2048]{1,0:T(8,128)(2,1)}, bf16[128,2048]{1,0:T(8,128)(2,1)}) custom-call(bf16[32,128,128]{2,1,0:T(8,128)(2,1)} %get-tuple-element.16.rmix_hbm, bf16[32,128,128]{2,1,0:T(8,128)(2,1)} %get-tuple-element.17.rkv_hbm), custom_call_target="tpu_custom_call" | custom-call | tf_op jit(solution)/shard_map/unpack/pallas_call | solution.py:584
